TPU v7x, 512 devices: a whole 4x4x16 slice. The times are simulated.
512 devices in a mesh: seq: 8 (over z_hi, x), chan: 64 (over z_lo, y, core).
Axes of the slice: x: 4, y: 4, z: 16 (z_hi: 2, z_lo: 8; z = z_hi * 8 + z_lo), core: 2. Of those that a mesh axis runs over, the one named last changes fastest.
Arguments:
- query_gate: bfloat16 [1024, 8192], P('chan', 'seq'), may hold values from -6 to 6
- key_gate: bfloat16 [1024, 8192], P('chan', 'seq'), may hold values from -6 to 6
- values: bfloat16 [1024, 8192], P('chan', 'seq'), may hold values from -6 to 6
- filters: float32 [256, 8192], P(None, ('seq', 'chan')), may hold values from -2 to 2
- out_grad: bfloat16 [1024, 8192], P('chan', 'seq'), may hold values from -6 to 6
Outputs:
- query_grad: bfloat16 [1024, 8192], P('chan', 'seq')
- key_grad: bfloat16 [1024, 8192], P('chan', 'seq')
- value_grad: bfloat16 [1024, 8192], P('chan', 'seq')
- filter_grad: float32 [256, 8192], P(None, ('seq', 'chan'))
All inputs are finite; a program needn't handle non-finite values.
Results may differ from a plain program's by a relative error of at most 0.0019.
Values sent between devices are 32-bit elements; how exact they have to be, the bound alone decides.
No kernel may reach another device: no remote copies, remote signals or barrier semaphores. Data moves between devices by JAX's collectives and lax.ppermute only.
A program may use at most 128 MiB of HBM per device.

v0:
```python
import jax
import jax.numpy as jnp
from jax import lax
from jax.sharding import PartitionSpec as P

HIGHEST = lax.Precision.HIGHEST
TWO_PI = 6.283185307179586


def angle_table(first_count, second_count, modulus):
    left_index = jnp.arange(first_count, dtype=jnp.int32)[:, None]
    right_index = jnp.arange(second_count, dtype=jnp.int32)[None, :]
    phases = (left_index * right_index % modulus).astype(jnp.float32) * (TWO_PI / modulus)
    return (jnp.cos(phases), jnp.sin(phases))


def split_size(length):
    for candidate in range(32, 1, -1):
        if length % candidate == 0 and length // candidate >= 128:
            return candidate
    return 1


def forward_transform(real_part, imag_part):
    length = real_part.shape[-1]
    radix_size = split_size(length)
    if radix_size == 1:
        cos_table, sin_table = angle_table(length, length, length)
        out_real = jnp.einsum(
            "...t,tk->...k", real_part, cos_table, precision=HIGHEST
        ) + jnp.einsum("...t,tk->...k", imag_part, sin_table, precision=HIGHEST)
        out_imag = jnp.einsum(
            "...t,tk->...k", imag_part, cos_table, precision=HIGHEST
        ) - jnp.einsum("...t,tk->...k", real_part, sin_table, precision=HIGHEST)
        return (out_real, out_imag)
    remainder = length // radix_size
    leading = real_part.shape[:-1]
    real_grid = real_part.reshape(leading + (radix_size, remainder))
    imag_grid = imag_part.reshape(leading + (radix_size, remainder))
    cos_table, sin_table = angle_table(radix_size, radix_size, radix_size)
    section_real = jnp.einsum(
        "...ab,ak->...kb", real_grid, cos_table, precision=HIGHEST
    ) + jnp.einsum("...ab,ak->...kb", imag_grid, sin_table, precision=HIGHEST)
    section_imag = jnp.einsum(
        "...ab,ak->...kb", imag_grid, cos_table, precision=HIGHEST
    ) - jnp.einsum("...ab,ak->...kb", real_grid, sin_table, precision=HIGHEST)
    twist_cos, twist_sin = angle_table(radix_size, remainder, length)
    turned_real = section_real * twist_cos + section_imag * twist_sin
    turned_imag = section_imag * twist_cos - section_real * twist_sin
    inner_real, inner_imag = forward_transform(turned_real, turned_imag)
    return (inner_real.reshape(leading + (length,)), inner_imag.reshape(leading + (length,)))


def inverse_transform(real_part, imag_part):
    length = real_part.shape[-1]
    radix_size = split_size(length)
    if radix_size == 1:
        cos_table, sin_table = angle_table(length, length, length)
        out_real = jnp.einsum(
            "...k,kt->...t", real_part, cos_table, precision=HIGHEST
        ) - jnp.einsum("...k,kt->...t", imag_part, sin_table, precision=HIGHEST)
        out_imag = jnp.einsum(
            "...k,kt->...t", real_part, sin_table, precision=HIGHEST
        ) + jnp.einsum("...k,kt->...t", imag_part, cos_table, precision=HIGHEST)
        return (out_real, out_imag)
    remainder = length // radix_size
    leading = real_part.shape[:-1]
    real_grid = real_part.reshape(leading + (radix_size, remainder))
    imag_grid = imag_part.reshape(leading + (radix_size, remainder))
    inner_real, inner_imag = inverse_transform(real_grid, imag_grid)
    twist_cos, twist_sin = angle_table(radix_size, remainder, length)
    turned_real = inner_real * twist_cos - inner_imag * twist_sin
    turned_imag = inner_real * twist_sin + inner_imag * twist_cos
    cos_table, sin_table = angle_table(radix_size, radix_size, radix_size)
    out_real = jnp.einsum(
        "...kb,ka->...ab", turned_real, cos_table, precision=HIGHEST
    ) - jnp.einsum("...kb,ka->...ab", turned_imag, sin_table, precision=HIGHEST)
    out_imag = jnp.einsum(
        "...kb,ka->...ab", turned_real, sin_table, precision=HIGHEST
    ) + jnp.einsum("...kb,ka->...ab", turned_imag, cos_table, precision=HIGHEST)
    return (out_real.reshape(leading + (length,)), out_imag.reshape(leading + (length,)))


def product_of(first_real, first_imag, second_real, second_imag, conjugate):
    if conjugate:
        second_imag = -second_imag
    return (
        first_real * second_real - first_imag * second_imag,
        first_real * second_imag + first_imag * second_real,
    )


def spectra_products(spec_real, spec_imag):
    conv_real, conv_imag = product_of(spec_real[0], spec_imag[0], spec_real[2], spec_imag[2], False)
    corr_real, corr_imag = product_of(spec_real[1], spec_imag[1], spec_real[2], spec_imag[2], True)
    taps_real, taps_imag = product_of(spec_real[1], spec_imag[1], spec_real[0], spec_imag[0], True)
    return (
        jnp.stack([conv_real, corr_real, taps_real]),
        jnp.stack([conv_imag, corr_imag, taps_imag]),
    )


def global_twist(position, block_len, radix_count, full_len):
    frequency = jnp.arange(radix_count, dtype=jnp.int32)[:, None]
    column_index = position * block_len + jnp.arange(block_len, dtype=jnp.int32)[None, :]
    phases = (frequency * column_index % full_len).astype(jnp.float32) * (TWO_PI / full_len)
    return (jnp.cos(phases), jnp.sin(phases))


def spread_forward(stacked_rows, seq_count, position):
    row_total, local_len = stacked_rows.shape
    block_len = local_len // seq_count
    full_len = 2 * local_len * seq_count
    row_grid = stacked_rows.reshape(row_total, seq_count, block_len)
    arrived = lax.all_to_all(row_grid, "seq", split_axis=1, concat_axis=1, tiled=True)
    cos_table, sin_table = angle_table(seq_count, 2 * seq_count, 2 * seq_count)
    section_real = jnp.einsum("kab,ac->kcb", arrived, cos_table, precision=HIGHEST)
    section_imag = -jnp.einsum("kab,ac->kcb", arrived, sin_table, precision=HIGHEST)
    twist_cos, twist_sin = global_twist(position, block_len, 2 * seq_count, full_len)
    turned_real = section_real * twist_cos + section_imag * twist_sin
    turned_imag = section_imag * twist_cos - section_real * twist_sin
    landed = lax.all_to_all(
        jnp.stack([turned_real, turned_imag]), "seq", split_axis=2, concat_axis=3, tiled=True
    )
    return forward_transform(landed[0], landed[1])


def spread_inverse(spec_real, spec_imag, seq_count, position):
    row_total = spec_real.shape[0]
    local_len = spec_real.shape[-1]
    block_len = local_len // seq_count
    full_len = 2 * local_len * seq_count
    back_real, back_imag = inverse_transform(spec_real, spec_imag)
    arrived = lax.all_to_all(
        jnp.stack([back_real, back_imag]), "seq", split_axis=3, concat_axis=2, tiled=True
    )
    twist_cos, twist_sin = global_twist(position, block_len, 2 * seq_count, full_len)
    turned_real = arrived[0] * twist_cos - arrived[1] * twist_sin
    turned_imag = arrived[0] * twist_sin + arrived[1] * twist_cos
    cos_table, sin_table = angle_table(2 * seq_count, seq_count, 2 * seq_count)
    row_values = (
        jnp.einsum("kcb,ca->kab", turned_real, cos_table, precision=HIGHEST)
        - jnp.einsum("kcb,ca->kab", turned_imag, sin_table, precision=HIGHEST)
    ) / full_len
    landed = lax.all_to_all(row_values, "seq", split_axis=1, concat_axis=2, tiled=True)
    return landed.reshape(row_total, local_len)


def on_device(query_gate, key_gate, values, filters, out_grad):
    channel_count, local_len = query_gate.shape
    seq_count = lax.axis_size("seq")
    chan_count = lax.axis_size("chan")
    filter_count, piece_len = filters.shape
    set_count = filter_count // channel_count
    first_row = lax.axis_index("chan") % set_count * channel_count
    gate_in = key_gate.astype(jnp.float32) * values.astype(jnp.float32)
    grad_conv = out_grad.astype(jnp.float32) * query_gate.astype(jnp.float32)
    all_rows = lax.all_gather(filters, "chan", axis=1, tiled=True)
    filter_taps = lax.dynamic_slice_in_dim(all_rows, first_row, channel_count, 0)
    stacked = jnp.stack([gate_in, grad_conv, filter_taps])
    position = lax.axis_index("seq")
    flat_rows = stacked.reshape(3 * channel_count, local_len)
    spec_real, spec_imag = spread_forward(flat_rows, seq_count, position)
    spec_shape = (3, channel_count) + spec_real.shape[1:]
    prod_real, prod_imag = spectra_products(
        spec_real.reshape(spec_shape), spec_imag.reshape(spec_shape)
    )
    flat_shape = (3 * channel_count,) + spec_real.shape[1:]
    landed = spread_inverse(
        prod_real.reshape(flat_shape), prod_imag.reshape(flat_shape), seq_count, position
    ).reshape(3, channel_count, local_len)
    conv_out = landed[0]
    grad_in = landed[1]
    filter_terms = landed[2]
    query_grad = (out_grad.astype(jnp.float32) * conv_out).astype(jnp.bfloat16)
    key_grad = (grad_in * values.astype(jnp.float32)).astype(jnp.bfloat16)
    value_grad = (grad_in * key_gate.astype(jnp.float32)).astype(jnp.bfloat16)
    group_size = channel_count * chan_count // filter_count
    grad_scale = 1.0 / jnp.sqrt(jnp.float32(local_len * seq_count * group_size))
    placed = lax.dynamic_update_slice_in_dim(
        jnp.zeros((filter_count, local_len), jnp.float32), filter_terms, first_row, 0
    )
    summed = lax.psum_scatter(placed, "chan", scatter_dimension=1, tiled=True)
    filter_grad = summed * grad_scale
    return (query_grad, key_grad, value_grad, filter_grad)


def solution(mesh):
    placed = (
        P("chan", "seq"),
        P("chan", "seq"),
        P("chan", "seq"),
        P(None, ("seq", "chan")),
        P("chan", "seq"),
    )
    return jax.shard_map(
        on_device,
        mesh=mesh,
        in_specs=placed,
        out_specs=(P("chan", "seq"), P("chan", "seq"), P("chan", "seq"), P(None, ("seq", "chan"))),
        check_vma=False,
    )
```

profile of v0, /device:TPU:1, one launch (start us, length us, event | category | flops | bytes accessed | tf_op | source)
XLA Modules:
  0.0 732.9 jit_solution(17508994716884536797)
XLA Ops:
  7.2 0.7 all-gather.2.cloned.1.call-update
  7.9 0.8 fusion.28
  8.7 126.4 %all-gather.2.cloned.1.call-done = f32[256,1024]{0,1:T(8,128)} async-done(((f32[256,16]{0,1:T(8,128)}), f32[256,1024]{0,1:T(8,128)}) %all-gather.2.cloned.1.call-update) | async-done | bytes 1048592 | tf_op jit(solution)/shard_map/all_gather | solution.py:158
  135.1 1.2 constant_dynamic-slice_fusion
  136.4 0.2 copy.55
  136.6 0.7 copy.56
  137.3 9.9 %all-to-all-start = ((f32[48,8,128]{2,0,1:T(8,128)}), f32[48,8,128]{2,0,1:T(8,128)S(1)}, u32[]{:S(2)}, u32[]{:S(2)}) async-start(f32[48,8,128]{2,0,1:T(8,128)} %copy.56), calls=%async_computation | async-start | bytes 393216 | tf_op jit(solution)/shard_map/all_to_all | solution.py:115
  147.3 0.1 fusion.94
  147.3 14.8 %all-to-all-done = f32[48,8,128]{2,0,1:T(8,128)S(1)} async-done(((f32[48,8,128]{2,0,1:T(8,128)}), f32[48,8,128]{2,0,1:T(8,128)S(1)}, u32[]{:S(2)}, u32[]{:S(2)}) %all-to-all-start) | async-done | bytes 196640 | tf_op jit(solution)/shard_map/all_to_all | solution.py:115
  162.2 0.6 convolution_negate_fusion
  162.8 0.6 add_bitcast_fusion
  163.5 1.1 copy.59
  164.6 3.5 all-to-all-start.1
  168.3 18.0 %all-to-all-done.1 = f32[2,48,16,128]{3,1,0,2:T(8,128)S(1)} async-done(((f32[2,48,16,128]{3,1,0,2:T(8,128)}), f32[2,48,16,128]{3,1,0,2:T(8,128)S(1)}, u32[]{:S(2)}, u32[]{:S(2)}) %all-to-all-start.1) | async-done | bytes 786464 | tf_op jit(solution)/shard_map/all_to_all | solution.py:122
  186.3 0.5 copy.94
  186.7 0.5 fusion.18
  187.3 0.5 fusion.17
  187.8 0.5 convolution_subtract_fusion.3
  188.3 0.5 convolution_add_fusion.3
  188.8 0.7 fusion.8
  189.5 0.7 fusion.4
  190.3 0.7 convolution_add_fusion.2
  191.0 0.1 squeeze.42
  191.1 0.1 squeeze.41
  191.2 0.1 squeeze.45
  191.2 0.7 convolution_subtract_fusion.2
  192.0 0.1 squeeze.43
  192.1 0.1 squeeze.44
  192.2 0.1 squeeze.46
  192.2 0.1 multiply_add_fusion.4
  192.4 0.2 pad_maximum_fusion.2
  192.5 0.3 reshape_reshape.13
  192.9 0.7 fusion.42
  193.6 0.7 fusion.36
  194.3 0.2 pad_maximum_fusion.3
  194.5 0.3 reshape_reshape.14
  194.8 0.7 convolution_subtract_fusion.1
  195.5 0.7 convolution_add_fusion.1
  196.3 0.5 fusion.27
  196.8 0.5 fusion.26
  197.3 0.5 fusion.1
  197.8 0.5 copy.77
  198.3 0.7 fusion
  199.0 1.4 copy.78
  200.3 2.3 fusion.207
  202.6 4.4 reshape.364
  207.0 23.9 %all_to_all.44 = f32[8,1,24576]{2,1,0:T(1,128)S(1)} all-to-all(f32[8,1,24576]{2,1,0:T(1,128)} %reshape.364), channel_id=1, replica_groups=mesh['seq'=8,'chan'=64] {'seq'}, dimensions={0} | all-to-all | bytes 1572864 | tf_op jit(solution)/shard_map/all_to_all | solution.py:134
  230.9 0.5 broadcast.346
  231.4 3.7 reduce
  235.1 4.5 reshape.365
  239.7 2.1 fusion.203
  241.7 1.5 copy.64
  243.2 0.5 copy.65
  243.8 0.4 fusion.13
  244.2 0.4 fusion.3
  244.6 22.3 %all_to_all.45 = f32[48,8,128]{2,0,1:T(8,128)S(1)} all-to-all(f32[48,8,128]{2,0,1:T(8,128)S(1)} %copy.66), channel_id=1, replica_groups=mesh['seq'=8,'chan'=64] {'seq'}, dimensions={1} | all-to-all | bytes 393216 | tf_op jit(solution)/shard_map/all_to_all | solution.py:145
  267.0 0.2 copy.79
  267.2 0.1 broadcast_in_dim.2
  267.2 4.8 dynamic_update_slice.3
  272.0 1.0 copy-done
  273.1 0.6 fusion.29
  273.7 0.6 fusion.30
  274.3 450.4 %reduce-scatter.2.cloned.1.call-done = f32[256,16]{0,1:T(8,128)} async-done(((f32[256,1024]{0,1:T(8,128)}), f32[256,16]{0,1:T(8,128)}) %reduce-scatter.2.cloned.1.call-update) | async-done | bytes 16400 | tf_op jit(solution)/shard_map/reduce_scatter | solution.py:183
  724.7 1.3 broadcast_multiply_fusion
  (19 shorter events, 0.4 us)
Async XLA Ops:
  7.2 128.0 %all-gather.2.cloned.1.call-start = ((), (), s32[]{:S(2)}) async-start(), calls=%async_computation.5 | async-start | bytes 1064960 | tf_op jit(solution)/shard_map/all_gather | solution.py:158
  137.3 24.8 %all-to-all-start = ((f32[48,8,128]{2,0,1:T(8,128)}), f32[48,8,128]{2,0,1:T(8,128)S(1)}, u32[]{:S(2)}, u32[]{:S(2)}) async-start(f32[48,8,128]{2,0,1:T(8,128)} %copy.56), calls=%async_computation | async-start | bytes 393216 | tf_op jit(solution)/shard_map/all_to_all | solution.py:115
  164.6 21.7 %all-to-all-start.1 = ((f32[2,48,16,128]{3,1,0,2:T(8,128)}), f32[2,48,16,128]{3,1,0,2:T(8,128)S(1)}, u32[]{:S(2)}, u32[]{:S(2)}) async-start(f32[2,48,16,128]{3,1,0,2:T(8,128)} %copy.59), calls=%async_computation.1 | async-start | bytes 1572864 | tf_op jit(solution)/shard_map/all_to_all | solution.py:122
  168.1 556.6 %reduce-scatter.2.cloned.1.call-start = ((), (), s32[]{:S(2)}) async-start(), calls=%async_computation.6 | async-start | bytes 1064960 | tf_op jit(solution)/shard_map/reduce_scatter | solution.py:183
  266.9 6.1 copy-start.1
  266.9 6.7 copy-start.2
  266.9 6.7 copy-start.3
  272.0 1.0 copy-start
Sparse Core Ops, SparseCore 0:
  10.2 124.9 all-gather.1
  273.2 451.5 reduce-scatter.1
where the time goes:
time: 742 us; the launch traced here: 733 us
  waiting for transfers between devices  610 us (82%)
  blocking collectives  46.3 us (6%)
  local copies, waits for them, and re-layouts  26.3 us (4%)
  between operations  14.5 us (2%)
  starting transfers between devices  13.6 us (2%)
  matrix products  11.9 us (2%)
  other arithmetic  10.1 us (1%)
    reduce_scatter x1, waiting for transfers between devices, on_device(): summed = lax.psum_scatter(placed, 'chan', scatter_dimension=1, tiled=True)  450 us
    all_gather x1, waiting for transfers between devices, on_device(): all_rows = lax.all_gather(filters, 'chan', axis=1, tiled=True)  126 us
    all_to_all x1, blocking collectives, spread_inverse(): lax.all_to_all(jnp.stack([back_real, back_imag]), 'seq', split_axis=3, co...  23.9 us
    all_to_all x1, blocking collectives, spread_inverse(): lax.all_to_all(row_values, 'seq', split_axis=1, concat_axis=2, tiled=True)  22.3 us
    all_to_all x1, waiting for transfers between devices, spread_forward(): lax.all_to_all(jnp.stack([turned_real, turned_imag]), 'seq', split_axis=2...  18 us
  transfers between devices with their start and end apart: 4, of which 4 were waited for; matrix products, arithmetic and copies ran while one was open for 0% of the time, Pallas kernels for 0%

commit v1 on v0

v1 whole, which is shorter than its diff:
```python
import ml_dtypes
import numpy as np
import jax
import jax.numpy as jnp
from jax import lax
from jax.experimental import pallas as pl
from jax.experimental.pallas import tpu as pltpu
from jax.sharding import Mesh
from jax.sharding import PartitionSpec as P

N = 16384
ROWS = 72
F32 = jnp.float32
BF16 = jnp.bfloat16
MSG = 18


def split_table(table):
    high = table.astype(ml_dtypes.bfloat16)
    low = (table - high.astype(np.float64)).astype(ml_dtypes.bfloat16)
    return high, low


def tables():
    k1 = np.arange(ROWS)
    live = (k1 <= 64).astype(np.float64)
    t1 = np.arange(64)
    t2 = np.arange(128)
    turn = 2 * np.pi / 128

    angle = turn * (k1[:, None] * t1[None, :] % 128)
    first = np.concatenate([live[:, None] * np.cos(angle), -live[:, None] * np.sin(angle)])
    high, low = split_table(first)
    first3 = np.concatenate([high, high, low], axis=1)

    taps3 = []
    for parity in range(2):
        part = np.tile(first[:, parity::2], (1, 4))
        high, low = split_table(part)
        taps3 += [high, high, low]
    taps3 = np.concatenate(taps3, axis=1)

    angle = 2 * np.pi / N * (k1[:, None] * t2[None, :] % N)
    twist = np.stack([live[:, None] * np.cos(angle), live[:, None] * np.sin(angle)]).astype(np.float32)

    angle = turn * (t2[:, None] * t2[None, :] % 128)
    cos, sin = np.cos(angle), np.sin(angle)
    second = np.block([[cos, -sin], [sin, cos]])
    high, low = split_table(second)
    second3 = np.concatenate([high, low, high], axis=0)

    weight = live * np.where((k1 == 0) | (k1 == 64), 1.0, 2.0) / N
    angle = turn * (t1[:, None] * k1[None, :] % 128)
    last = np.concatenate([weight * np.cos(angle), weight * np.sin(angle)], axis=1)
    last3, lags3 = [], []
    for half in range(2):
        part = last[half * 32 : half * 32 + 32]
        high, low = split_table(part)
        last3.append(np.concatenate([high, high, low], axis=1))
        part = np.concatenate([np.tile(part[parity::2].T, (1, 8)) for parity in range(2)], axis=1)
        high, low = split_table(part)
        lags3.append(np.concatenate([high, low, high], axis=0))
    return first3, taps3, twist, second3, np.stack(last3), np.stack(lags3)


def halves(x):
    high = x.astype(BF16)
    return high, (x - high.astype(F32)).astype(BF16)


def lanes3(x):
    high, low = halves(x)
    return jnp.concatenate([high, low, high], axis=1)


def lanes3_table_last(x):
    high, low = halves(x)
    return jnp.concatenate([high, high, low], axis=1)


def rows3(x):
    high, low = halves(x)
    return jnp.concatenate([high, low, high], axis=0)


def mm(a, b):
    return jnp.dot(a, b, preferred_element_type=F32)


def turned(x_re, x_im, twist_ref):
    cos, sin = twist_ref[0], twist_ref[1]
    return x_re * cos + x_im * sin, x_im * cos - x_re * sin


def second_stage(stacked, second_ref):
    return mm(lanes3_table_last(stacked), second_ref[...])


def lane_group(width, rows):
    return lax.broadcasted_iota(jnp.int32, (rows, 128), 1) // width


def pack_kernel(q_ref, k_ref, v_ref, g_ref, f_ref, out_ref):
    gate_in = k_ref[...].astype(F32) * v_ref[...].astype(F32)
    grad_conv = g_ref[...].astype(F32) * q_ref[...].astype(F32)
    for copy in range(2):
        base = copy * 16 * MSG
        for j in range(8):
            cols = slice(j * 128, j * 128 + 128)
            out_ref[pl.ds(base + j, 16, stride=MSG), :] = gate_in[:, cols]
            out_ref[pl.ds(base + 8 + j, 16, stride=MSG), :] = grad_conv[:, cols]
    for high in range(2):
        taps = jnp.concatenate(
            [f_ref[(high * 8 + m) * 16 : (high * 8 + m) * 16 + 16, :] for m in range(8)], axis=1
        )
        for copy in range(2):
            out_ref[pl.ds(copy * 16 * MSG + 16 + high, 16, stride=MSG), :] = taps


def forward_kernel(half_ref, in_ref, first_ref, twist_ref, second_ref, lags_ref, spec_ref, out_ref, taps_t, lags_t):
    columns = []
    for array in range(2):
        for chan in range(4):
            tiles = [
                in_ref[(block * 4 + chan) * MSG + array * 8 : (block * 4 + chan) * MSG + array * 8 + 8, :]
                for block in range(8)
            ]
            columns.append(jnp.concatenate(tiles, axis=0))
    signals = jnp.concatenate(columns, axis=1)
    section = mm(first_ref[...], rows3(signals))
    stacked = []
    for s in range(8):
        cols = slice(s * 128, s * 128 + 128)
        re, im = turned(section[:ROWS, cols], section[ROWS:, cols], twist_ref)
        stacked.append(jnp.concatenate([re, im], axis=1))
    spec = second_stage(jnp.concatenate(stacked, axis=0), second_ref)
    spec_ref[...] = spec

    sum_re = jnp.zeros((ROWS, 128), F32)
    sum_im = jnp.zeros((ROWS, 128), F32)
    for chan in range(4):
        x = spec[chan * ROWS : chan * ROWS + ROWS]
        g = spec[(4 + chan) * ROWS : (4 + chan) * ROWS + ROWS]
        sum_re += g[:, :128] * x[:, :128] + g[:, 128:] * x[:, 128:]
        sum_im += g[:, :128] * x[:, 128:] - g[:, 128:] * x[:, :128]
    back = second_stage(jnp.concatenate([sum_re, sum_im], axis=1), second_ref)
    re, im = turned(back[:, :128], back[:, 128:], twist_ref)
    flipped = jnp.concatenate([re, im], axis=0).T
    lags = mm(lanes3_table_last(flipped), lags_ref[half_ref[0]]) * np.float32(1.0 / np.sqrt(32768.0))
    lags_t[:128, :] = lags[:, :128]
    lags_t[128:, :] = lags[:, 128:]

    group8 = lane_group(16, 8)
    group4 = lane_group(32, 8)
    zero = jnp.zeros((8, 128), F32)
    for high in range(2):
        taps = in_ref[pl.ds(16 + high, 32, stride=MSG), :]
        taps_t[...] = jnp.concatenate([taps] * 4, axis=0).T
        base = high * 64
        for b in range(4):
            row = zero
            for a in range(4):
                row = jnp.where(group4 == a, taps_t[pl.ds(4 * a + b, 8, stride=16), :], row)
            out_ref[pl.ds(base + b, 8, stride=8), :] = row
        for b in range(2):
            row = zero
            for a in range(8):
                row = jnp.where(group8 == a, lags_t[pl.ds(high * 128 + 2 * a + b, 8, stride=16), :], row)
            out_ref[pl.ds(base + 4 + b, 8, stride=8), :] = row
        for b in range(2):
            out_ref[pl.ds(base + 6 + b, 8, stride=8), :] = zero


def backward_kernel(half_ref, in_ref, spec_ref, taps_ref, twist_ref, second_ref, last_ref, out_ref, taps_t, lags_t):
    group8 = lane_group(16, 16)
    group4 = lane_group(32, 16)
    for b in range(4):
        row = in_ref[pl.ds(b, 16, stride=8), :]
        for a in range(4):
            taps_t[pl.ds(4 * a + b, 16, stride=16), :] = jnp.where(group4 == a, row, 0.0)
    for b in range(2):
        row = in_ref[pl.ds(4 + b, 16, stride=8), :]
        for a in range(8):
            lags_t[pl.ds(2 * a + b, 16, stride=16), :] = jnp.where(group8 == a, row, 0.0)
    for high in range(2):
        flipped = lags_t[high * 128 : high * 128 + 128, :].T
        total = flipped[:16]
        for a in range(1, 8):
            total += flipped[a * 16 : a * 16 + 16]
        out_ref[pl.ds(16 + high, 16, stride=MSG), :] = total

    taps = jnp.concatenate([lanes3(taps_t[:128, :]), lanes3(taps_t[128:, :])], axis=1)
    section = lax.dot_general(
        taps_ref[...], taps, (((1,), (1,)), ((), ())), preferred_element_type=F32
    )
    re, im = turned(section[:ROWS], section[ROWS:], twist_ref)
    filt = second_stage(jnp.concatenate([re, im], axis=1), second_ref)
    h_re, h_im = filt[:, :128], filt[:, 128:]

    products = []
    for s in range(8):
        re, im = spec_ref[s * ROWS : s * ROWS + ROWS, :128], spec_ref[s * ROWS : s * ROWS + ROWS, 128:]
        if s < 4:
            products.append(jnp.concatenate([re * h_re - im * h_im, -(re * h_im + im * h_re)], axis=1))
        else:
            products.append(jnp.concatenate([re * h_re + im * h_im, re * h_im - im * h_re], axis=1))
    back = second_stage(jnp.concatenate(products, axis=0), second_ref)
    columns = []
    for s in range(8):
        part = back[s * ROWS : s * ROWS + ROWS]
        re, im = turned(part[:, :128], part[:, 128:], twist_ref)
        columns.append(jnp.concatenate([re, im], axis=0))
    landed = mm(last_ref[half_ref[0]], rows3(jnp.concatenate(columns, axis=1)))
    for s in range(8):
        array, chan = s // 4, s % 4
        for block in range(4):
            start = (block * 4 + chan) * MSG + array * 8
            out_ref[start : start + 8, :] = landed[block * 8 : block * 8 + 8, s * 128 : s * 128 + 128]


def finish_kernel(in_ref, k_ref, v_ref, g_ref, q_out, k_out, v_out, f_out):
    for j in range(8):
        cols = slice(j * 128, j * 128 + 128)
        conv = in_ref[pl.ds(j, 16, stride=MSG), :]
        grad = in_ref[pl.ds(8 + j, 16, stride=MSG), :]
        q_out[:, cols] = (g_ref[:, cols].astype(F32) * conv).astype(BF16)
        k_out[:, cols] = (grad * v_ref[:, cols].astype(F32)).astype(BF16)
        v_out[:, cols] = (grad * k_ref[:, cols].astype(F32)).astype(BF16)
    for high in range(2):
        rows = in_ref[pl.ds(16 + high, 16, stride=MSG), :]
        for m in range(8):
            start = (high * 8 + m) * 16
            f_out[start : start + 16, :] = rows[:, m * 16 : m * 16 + 16]


SMEM = pl.BlockSpec(memory_space=pltpu.SMEM)
VMEM = pl.BlockSpec(memory_space=pltpu.VMEM)
PARAMS = pltpu.CompilerParams(vmem_limit_bytes=32 * 1024 * 1024)


def shape(*dims, dtype=F32):
    return jax.ShapeDtypeStruct(dims, dtype)


def on_device(q, k, v, filters, g):
    first3, taps3, twist, second3, last3, lags3 = (jnp.asarray(t) for t in tables())
    half = lax.axis_index("zh").astype(jnp.int32).reshape(1)

    packed = pl.pallas_call(
        pack_kernel, out_shape=shape(32 * MSG, 128), in_specs=[VMEM] * 5, out_specs=VMEM, compiler_params=PARAMS
    )(q, k, v, g, filters)
    arrived = lax.all_to_all(
        packed.reshape(32, MSG // 2, 2, 128), ("zh", "x", "zg"), split_axis=0, concat_axis=0, tiled=True
    ).reshape(32 * MSG, 128)

    spec, sent = pl.pallas_call(
        forward_kernel,
        out_shape=(shape(8 * ROWS, 256), shape(128, 128)),
        in_specs=[SMEM] + [VMEM] * 5,
        out_specs=(VMEM, VMEM),
        scratch_shapes=[pltpu.VMEM((128, 128), F32), pltpu.VMEM((256, 128), F32)],
        compiler_params=PARAMS,
    )(half, arrived, first3, twist, second3, lags3)
    swapped = lax.all_to_all(
        sent.reshape(16, 8, 128), ("zb", "y", "core"), split_axis=0, concat_axis=0, tiled=True
    ).reshape(128, 128)

    landed = pl.pallas_call(
        backward_kernel,
        out_shape=shape(16 * MSG, 128),
        in_specs=[SMEM] + [VMEM] * 6,
        out_specs=VMEM,
        scratch_shapes=[pltpu.VMEM((256, 128), F32), pltpu.VMEM((256, 128), F32)],
        compiler_params=PARAMS,
    )(half, swapped, spec, taps3, twist, second3, last3)
    home = lax.all_to_all(
        landed.reshape(16, MSG // 2, 2, 128), ("x", "zg"), split_axis=0, concat_axis=0, tiled=True
    ).reshape(16 * MSG, 128)

    out = shape(*q.shape, dtype=BF16)
    return pl.pallas_call(
        finish_kernel,
        out_shape=(out, out, out, shape(*filters.shape)),
        in_specs=[VMEM] * 4,
        out_specs=(VMEM,) * 4,
        compiler_params=PARAMS,
    )(home, k, v, g)


def solution(mesh):
    fine = Mesh(mesh.devices.reshape(2, 4, 4, 2, 4, 2), ("zh", "x", "zg", "zb", "y", "core"))
    seq, chan = ("zh", "x"), ("zg", "zb", "y", "core")
    gates, taps = P(chan, seq), P(None, seq + chan)
    return jax.shard_map(
        on_device,
        mesh=fine,
        in_specs=(gates, gates, gates, taps, gates),
        out_specs=(gates, gates, gates, taps),
        check_vma=False,
    )
```

time: 742 us -> 78.2 us (0.11); the launches traced: 733 us -> 77.8 us
  waiting for transfers between devices: 610 us -> 19.1 us
  local copies, waits for them, and re-layouts: 26.3 us -> 1.56 us
  between operations: 14.5 us -> 0.75 us
  blocking collectives: 46.3 us -> 33.8 us
  matrix products: 11.9 us -> 0 us
  other arithmetic: 10.1 us -> 0 us
    reduce_scatter x1 -> x0, waiting for transfers between devices: 450 us -> none  [on_device(): summed = lax.psum_scatter(placed, 'chan', scatter_dimension=1, tiled=True)]
    all_gather x1 -> x0, waiting for transfers between devices: 126 us -> none  [on_device(): all_rows = lax.all_gather(filters, 'chan', axis=1, tiled=True)]
    all_to_all x2 -> x1, waiting for transfers between devices: 32.9 us -> 19.1 us  [on_device(): lax.all_to_all(packed.reshape(32, MSG // 2, 2, 128), ('zh', 'x', 'zg'), s...]
    all_to_all x2, blocking collectives: 46.3 us -> 33.8 us  [the longest x1 18.1 us: on_device(): lax.all_to_all(landed.reshape(16, MSG // 2, 2, 128), ('x', 'zg'), split_a...]
    dot_general x20 -> x0, matrix products: 11.9 us -> none  [the longest x1 0.72 us: forward_transform(): jnp.einsum('...t,tk->...k', imag_part, sin_table, precision=HIGHEST)]
    unnamed x11 -> x21, local copies, waits for them, and re-layouts: 9.93 us -> 0.89 us
    all_to_all x2 -> x1, starting transfers between devices: 13.5 us -> 18.6 us  [on_device(): lax.all_to_all(packed.reshape(32, MSG // 2, 2, 128), ('zh', 'x', 'zg'), s...]
  transfers between devices with their start and end apart: 4 -> 1, of which waited for: 4 -> 1; matrix products, arithmetic and copies ran while one was open for 0% -> 0% of each run, Pallas kernels for 0% -> 0%
where the time goes in v1:
time: 78.2 us; the launch traced here: 77.8 us
  blocking collectives  33.8 us (43%)
  waiting for transfers between devices  19.1 us (24%)
  starting transfers between devices  18.6 us (24%)
  Pallas kernels  3.97 us (5%)
  local copies, waits for them, and re-layouts  1.56 us (2%)
    all_to_all x1, waiting for transfers between devices, on_device(): lax.all_to_all(packed.reshape(32, MSG // 2, 2, 128), ('zh', 'x', 'zg'), s...  19.1 us
    all_to_all x1, starting transfers between devices, on_device(): lax.all_to_all(packed.reshape(32, MSG // 2, 2, 128), ('zh', 'x', 'zg'), s...  18.6 us
    all_to_all x1, blocking collectives, on_device(): lax.all_to_all(landed.reshape(16, MSG // 2, 2, 128), ('x', 'zg'), split_a...  18.1 us
    all_to_all x1, blocking collectives, on_device(): lax.all_to_all(sent.reshape(16, 8, 128), ('zb', 'y', 'core'), split_axis=...  15.7 us
  transfers between devices with their start and end apart: 1, of which 1 were waited for; matrix products, arithmetic and copies ran while one was open for 0% of the time, Pallas kernels for 0%

profile of v1, /device:TPU:1, one launch (start us, length us, event | category | flops | bytes accessed | tf_op | source)
XLA Modules:
  0.0 77.8 jit_solution(3104740085209092874)
XLA Ops:
  0.6 0.0 copy-start.6
  0.6 0.0 copy-start.5
  0.7 0.0 copy-start.4
  0.7 0.0 copy-start.9
  0.7 0.8 %copy.15.f_ref = f32[256,16]{1,0:T(8,128)S(1)} copy(f32[256,16]{0,1:T(8,128)} %param.14) | data formatting | bytes 32768 | tf_op args[3]
  1.5 0.0 copy-done.6
  1.5 0.0 copy-done.5
  1.5 0.0 copy-done.4
  1.5 0.0 copy-done.9
  1.5 0.0 copy-start.1
  1.6 0.8 %shard_map.138 = f32[576,128]{1,0:T(8,128)} custom-call(bf16[16,1024]{1,0:T(8,128)(2,1)S(1)} %copy-done.9, bf16[16,1024]{1,0:T(8,128)(2,1)S(1)} %copy-done.4, bf16[16,1024]{1,0:T(8,128)(2,1)S(1)} %copy-done.5, bf16[16,1024]{1,0:T(8,128)(2,1)S(1)} %copy-done.6, f32[256,16]{1,0:T(8,128)S(1)} %copy.15.f_ref), custom_call_target="tpu_custom_call" | custom-call | tf_op jit(solution)/shard_map/pallas_call | solution.py:249
  2.4 0.0 copy-start
  2.4 0.0 copy-start.2
  2.4 0.0 copy-start.7
  2.4 18.6 %all-to-all-start = ((f32[32,9,2,128]{3,2,1,0:T(2,128)}), f32[32,9,2,128]{3,2,1,0:T(2,128)S(1)}, u32[]{:S(2)}, u32[]{:S(2)}) async-start(f32[32,9,2,128]{3,2,1,0:T(2,128)} %bitcast.1), calls=%async_computation | async-start | bytes 589824 | tf_op jit(solution)/shard_map/all_to_all | solution.py:252
  21.0 19.1 %all-to-all-done = f32[32,9,2,128]{3,2,1,0:T(2,128)S(1)} async-done(((f32[32,9,2,128]{3,2,1,0:T(2,128)}), f32[32,9,2,128]{3,2,1,0:T(2,128)S(1)}, u32[]{:S(2)}, u32[]{:S(2)}) %all-to-all-start) | async-done | bytes 294944 | tf_op jit(solution)/shard_map/all_to_all | solution.py:252
  40.2 0.0 copy-done.1
  40.2 0.0 copy-done
  40.2 0.0 copy-done.2
  40.2 0.0 copy-done.7
  40.2 0.0 copy-start.3
  40.2 1.3 %shard_map.139 = (f32[576,256]{1,0:T(8,128)S(1)}, f32[128,128]{1,0:T(8,128)S(1)}) custom-call(s32[1]{0:T(128)} %bitcast.half_ref, f32[576,128]{1,0:T(8,128)S(1)} %bitcast.7, bf16[144,192]{1,0:T(8,128)(2,1)S(1)} %copy-done.7, f32[2,72,128]{2,1,0:T(8,128)S(1)} %copy-done.2, bf16[768,256]{1,0:T(8,128)(2,1)S(1)} %copy-done, bf16[2,432,256]{2,1,0:T(8,128)(2,1)S(1)} %copy-done.1), custom_call_target="tpu_custom_call" | custom-call | tf_op jit(solution)/shard_map/pallas_call | solution.py:256
  41.5 0.0 copy-start.8
  41.5 15.7 %all_to_all.15 = f32[16,8,128]{2,1,0:T(8,128)S(1)} all-to-all(f32[16,8,128]{2,1,0:T(8,128)S(1)} %bitcast.11), channel_id=1, replica_groups=mesh['zh'=2,'x'=4,'zg'=4,'zb'=2,'y'=4,'core'=2] {'zb','y','core'}, dimensions={0} | all-to-all | bytes 131072 | tf_op jit(solution)/shard_map/all_to_all | solution.py:264
  57.2 0.0 copy-done.3
  57.2 0.0 copy-done.8
  57.2 1.2 %shard_map.140 = f32[288,128]{1,0:T(8,128)S(1)} custom-call(s32[1]{0:T(128)} %bitcast.half_ref, f32[128,128]{1,0:T(8,128)S(1)} %bitcast.10, f32[576,256]{1,0:T(8,128)S(1)} %get-tuple-element.7.spec_ref, bf16[144,768]{1,0:T(8,128)(2,1)S(1)} %copy-done.3, f32[2,72,128]{2,1,0:T(8,128)S(1)} %copy-done.2, bf16[768,256]{1,0:T(8,128)(2,1)S(1)} %copy-done, ...), custom_call_target="tpu_custom_call" | custom-call | tf_op jit(solution)/shard_map/pallas_call | solution.py:268
  58.4 18.1 %all_to_all.16 = f32[16,9,2,128]{3,2,1,0:T(2,128)S(1)} all-to-all(f32[16,9,2,128]{3,2,1,0:T(2,128)S(1)} %bitcast.9), channel_id=1, replica_groups=mesh['zh'=2,'x'=4,'zg'=4,'zb'=2,'y'=4,'core'=2] {'x','zg'}, dimensions={0} | all-to-all | bytes 294912 | tf_op jit(solution)/shard_map/all_to_all | solution.py:276
  76.5 0.7 shard_map.141
  77.2 0.7 copy.16
Async XLA Ops:
  0.6 0.9 %copy-start.6 = (bf16[16,1024]{1,0:T(8,128)(2,1)S(1)}, bf16[16,1024]{1,0:T(8,128)(2,1)}, u32[]{:S(2)}) copy-start(bf16[16,1024]{1,0:T(8,128)(2,1)} %g_ref.3) | copy-start | bytes 98308
  0.6 0.9 %copy-start.5 = (bf16[16,1024]{1,0:T(8,128)(2,1)S(1)}, bf16[16,1024]{1,0:T(8,128)(2,1)}, u32[]{:S(2)}) copy-start(bf16[16,1024]{1,0:T(8,128)(2,1)} %v_ref.3) | copy-start | bytes 98308
  0.7 0.9 %copy-start.4 = (bf16[16,1024]{1,0:T(8,128)(2,1)S(1)}, bf16[16,1024]{1,0:T(8,128)(2,1)}, u32[]{:S(2)}) copy-start(bf16[16,1024]{1,0:T(8,128)(2,1)} %k_ref.3) | copy-start | bytes 98308
  0.7 0.9 %copy-start.9 = (bf16[16,1024]{1,0:T(8,128)(2,1)S(1)}, bf16[16,1024]{1,0:T(8,128)(2,1)}, u32[]{:S(2)}) copy-start(bf16[16,1024]{1,0:T(8,128)(2,1)} %q_ref.1) | copy-start | bytes 98308
  1.5 38.6 %copy-start.1 = (bf16[2,432,256]{2,1,0:T(8,128)(2,1)S(1)}, bf16[2,432,256]{2,1,0:T(8,128)(2,1)}, u32[]{:S(2)}) copy-start(bf16[2,432,256]{2,1,0:T(8,128)(2,1)} %constant.23.clone.lags_ref) | copy-start | bytes 1327108
  2.4 37.8 %copy-start = (bf16[768,256]{1,0:T(8,128)(2,1)S(1)}, bf16[768,256]{1,0:T(8,128)(2,1)}, u32[]{:S(2)}) copy-start(bf16[768,256]{1,0:T(8,128)(2,1)} %constant.21.clone.second_ref) | copy-start | bytes 1179652
  2.4 37.8 %copy-start.2 = (f32[2,72,128]{2,1,0:T(8,128)S(1)}, f32[2,72,128]{2,1,0:T(8,128)}, u32[]{:S(2)}) copy-start(f32[2,72,128]{2,1,0:T(8,128)} %constant.20.clone.twist_ref) | copy-start | bytes 221188
  2.4 37.8 %copy-start.7 = (bf16[144,192]{1,0:T(8,128)(2,1)S(1)}, bf16[144,192]{1,0:T(8,128)(2,1)}, u32[]{:S(2)}) copy-start(bf16[144,192]{1,0:T(8,128)(2,1)} %constant.18.clone.first_ref) | copy-start | bytes 165892
  2.4 37.8 %all-to-all-start = ((f32[32,9,2,128]{3,2,1,0:T(2,128)}), f32[32,9,2,128]{3,2,1,0:T(2,128)S(1)}, u32[]{:S(2)}, u32[]{:S(2)}) async-start(f32[32,9,2,128]{3,2,1,0:T(2,128)} %bitcast.1), calls=%async_computation | async-start | bytes 589824 | tf_op jit(solution)/shard_map/all_to_all | solution.py:252
  40.2 17.0 %copy-start.3 = (bf16[144,768]{1,0:T(8,128)(2,1)S(1)}, bf16[144,768]{1,0:T(8,128)(2,1)}, u32[]{:S(2)}) copy-start(bf16[144,768]{1,0:T(8,128)(2,1)} %constant.19.clone.taps_ref) | copy-start | bytes 663556
  41.5 15.7 %copy-start.8 = (bf16[2,32,432]{2,1,0:T(8,128)(2,1)S(1)}, bf16[2,32,432]{2,1,0:T(8,128)(2,1)}, u32[]{:S(2)}) copy-start(bf16[2,32,432]{2,1,0:T(8,128)(2,1)} %constant.22.clone.last_ref) | copy-start | bytes 165892

commit v2 on v1

--- a/solution.py
+++ b/solution.py
@@ -15,6 +15,10 @@
 MSG = 18
 
 
+def half_of(group, window):
+    return window ^ (group // 2)
+
+
 def split_table(table):
     high = table.astype(ml_dtypes.bfloat16)
     low = (table - high.astype(np.float64)).astype(ml_dtypes.bfloat16)
@@ -54,10 +58,11 @@
     last = np.concatenate([weight * np.cos(angle), weight * np.sin(angle)], axis=1)
     last3, lags3 = [], []
     for half in range(2):
-        part = last[half * 32 : half * 32 + 32]
-        high, low = split_table(part)
+        high, low = split_table(last[half * 32 : half * 32 + 32])
         last3.append(np.concatenate([high, high, low], axis=1))
-        part = np.concatenate([np.tile(part[parity::2].T, (1, 8)) for parity in range(2)], axis=1)
+    for window in range(2):
+        rows = [half_of(group, window) * 32 + x * 8 + group * 2 for x in range(4) for group in range(4)]
+        part = np.concatenate([np.tile(last[np.array(rows) + parity].T, (1, 8)) for parity in range(2)], axis=1)
         high, low = split_table(part)
         lags3.append(np.concatenate([high, low, high], axis=0))
     return first3, taps3, twist, second3, np.stack(last3), np.stack(lags3)
@@ -100,7 +105,14 @@
     return lax.broadcasted_iota(jnp.int32, (rows, 128), 1) // width
 
 
-def pack_kernel(q_ref, k_ref, v_ref, g_ref, f_ref, out_ref):
+def pack_kernel(q_hbm, k_hbm, v_hbm, g_hbm, f_hbm, out_ref, q_ref, k_ref, v_ref, g_ref, f_ref, sems):
+    sources = (f_hbm, k_hbm, v_hbm, g_hbm, q_hbm)
+    targets = (f_ref, k_ref, v_ref, g_ref, q_ref)
+    copies = [pltpu.make_async_copy(source, target, sems.at[i]) for i, (source, target) in enumerate(zip(sources, targets))]
+    for copy in copies:
+        copy.start()
+    for copy in copies:
+        copy.wait()
     gate_in = k_ref[...].astype(F32) * v_ref[...].astype(F32)
     grad_conv = g_ref[...].astype(F32) * q_ref[...].astype(F32)
     for copy in range(2):
@@ -110,14 +122,13 @@
             out_ref[pl.ds(base + j, 16, stride=MSG), :] = gate_in[:, cols]
             out_ref[pl.ds(base + 8 + j, 16, stride=MSG), :] = grad_conv[:, cols]
     for high in range(2):
-        taps = jnp.concatenate(
-            [f_ref[(high * 8 + m) * 16 : (high * 8 + m) * 16 + 16, :] for m in range(8)], axis=1
-        )
+        flipped = f_ref[:, high * 128 : high * 128 + 128].T
+        taps = jnp.concatenate([flipped[m * 16 : m * 16 + 16, :] for m in range(8)], axis=1)
         for copy in range(2):
             out_ref[pl.ds(copy * 16 * MSG + 16 + high, 16, stride=MSG), :] = taps
 
 
-def forward_kernel(half_ref, in_ref, first_ref, twist_ref, second_ref, lags_ref, spec_ref, out_ref, taps_t, lags_t):
+def forward_kernel(window_ref, in_ref, first_ref, twist_ref, second_ref, lags_ref, spec_ref, out_ref, taps_t, lags_t):
     columns = []
     for array in range(2):
         for chan in range(4):
@@ -146,7 +157,7 @@
     back = second_stage(jnp.concatenate([sum_re, sum_im], axis=1), second_ref)
     re, im = turned(back[:, :128], back[:, 128:], twist_ref)
     flipped = jnp.concatenate([re, im], axis=0).T
-    lags = mm(lanes3_table_last(flipped), lags_ref[half_ref[0]]) * np.float32(1.0 / np.sqrt(32768.0))
+    lags = mm(lanes3_table_last(flipped), lags_ref[window_ref[0]]) * np.float32(1.0 / np.sqrt(32768.0))
     lags_t[:128, :] = lags[:, :128]
     lags_t[128:, :] = lags[:, 128:]
 
@@ -171,7 +182,7 @@
             out_ref[pl.ds(base + 6 + b, 8, stride=8), :] = zero
 
 
-def backward_kernel(half_ref, in_ref, spec_ref, taps_ref, twist_ref, second_ref, last_ref, out_ref, taps_t, lags_t):
+def backward_kernel(window_ref, in_ref, spec_ref, taps_ref, twist_ref, second_ref, last_ref, out_ref, taps_t, lags_t):
     group8 = lane_group(16, 16)
     group4 = lane_group(32, 16)
     for b in range(4):
@@ -210,12 +221,14 @@
         part = back[s * ROWS : s * ROWS + ROWS]
         re, im = turned(part[:, :128], part[:, 128:], twist_ref)
         columns.append(jnp.concatenate([re, im], axis=0))
-    landed = mm(last_ref[half_ref[0]], rows3(jnp.concatenate(columns, axis=1)))
-    for s in range(8):
-        array, chan = s // 4, s % 4
-        for block in range(4):
-            start = (block * 4 + chan) * MSG + array * 8
-            out_ref[start : start + 8, :] = landed[block * 8 : block * 8 + 8, s * 128 : s * 128 + 128]
+    for pair in range(2):
+        order = [array * 4 + pair * 2 + chan for array in range(2) for chan in range(2)]
+        landed = mm(last_ref[window_ref[0] ^ pair], rows3(jnp.concatenate([columns[s] for s in order], axis=1)))
+        for i, s in enumerate(order):
+            array, chan = s // 4, s % 4
+            for block in range(4):
+                start = (block * 4 + chan) * MSG + array * 8
+                out_ref[start : start + 8, :] = landed[block * 8 : block * 8 + 8, i * 128 : i * 128 + 128]
 
 
 def finish_kernel(in_ref, k_ref, v_ref, g_ref, q_out, k_out, v_out, f_out):
@@ -227,28 +240,40 @@
         k_out[:, cols] = (grad * v_ref[:, cols].astype(F32)).astype(BF16)
         v_out[:, cols] = (grad * k_ref[:, cols].astype(F32)).astype(BF16)
     for high in range(2):
-        rows = in_ref[pl.ds(16 + high, 16, stride=MSG), :]
-        for m in range(8):
-            start = (high * 8 + m) * 16
-            f_out[start : start + 16, :] = rows[:, m * 16 : m * 16 + 16]
+        flipped = in_ref[pl.ds(16 + high, 16, stride=MSG), :].T
+        f_out[:, high * 128 : high * 128 + 128] = jnp.concatenate(
+            [flipped[m * 16 : m * 16 + 16, :] for m in range(8)], axis=1
+        )
 
 
 SMEM = pl.BlockSpec(memory_space=pltpu.SMEM)
+HBM = pl.BlockSpec(memory_space=pltpu.HBM)
 VMEM = pl.BlockSpec(memory_space=pltpu.VMEM)
 PARAMS = pltpu.CompilerParams(vmem_limit_bytes=32 * 1024 * 1024)
 
 
+WINDOWS = [
+    [half_of(group, window) * 16 + x * 4 + group for x in range(4) for group in range(4)] for window in range(2)
+]
+
+
 def shape(*dims, dtype=F32):
     return jax.ShapeDtypeStruct(dims, dtype)
 
 
 def on_device(q, k, v, filters, g):
     first3, taps3, twist, second3, last3, lags3 = (jnp.asarray(t) for t in tables())
-    half = lax.axis_index("zh").astype(jnp.int32).reshape(1)
+    window = (lax.axis_index("zh") ^ (lax.axis_index("zg") // 2)).astype(jnp.int32).reshape(1)
 
     packed = pl.pallas_call(
-        pack_kernel, out_shape=shape(32 * MSG, 128), in_specs=[VMEM] * 5, out_specs=VMEM, compiler_params=PARAMS
-    )(q, k, v, g, filters)
+        pack_kernel,
+        out_shape=shape(32 * MSG, 128),
+        in_specs=[HBM] * 5,
+        out_specs=VMEM,
+        scratch_shapes=[pltpu.VMEM(q.shape, BF16)] * 4
+        + [pltpu.VMEM(filters.shape[::-1], F32), pltpu.SemaphoreType.DMA((5,))],
+        compiler_params=pltpu.CompilerParams(vmem_limit_bytes=60 * 1024 * 1024),
+    )(q, k, v, g, filters.T)
     arrived = lax.all_to_all(
         packed.reshape(32, MSG // 2, 2, 128), ("zh", "x", "zg"), split_axis=0, concat_axis=0, tiled=True
     ).reshape(32 * MSG, 128)
@@ -260,7 +285,7 @@
         out_specs=(VMEM, VMEM),
         scratch_shapes=[pltpu.VMEM((128, 128), F32), pltpu.VMEM((256, 128), F32)],
         compiler_params=PARAMS,
-    )(half, arrived, first3, twist, second3, lags3)
+    )(window, arrived, first3, twist, second3, lags3)
     swapped = lax.all_to_all(
         sent.reshape(16, 8, 128), ("zb", "y", "core"), split_axis=0, concat_axis=0, tiled=True
     ).reshape(128, 128)
@@ -272,19 +297,25 @@
         out_specs=VMEM,
         scratch_shapes=[pltpu.VMEM((256, 128), F32), pltpu.VMEM((256, 128), F32)],
         compiler_params=PARAMS,
-    )(half, swapped, spec, taps3, twist, second3, last3)
+    )(window, swapped, spec, taps3, twist, second3, last3)
     home = lax.all_to_all(
-        landed.reshape(16, MSG // 2, 2, 128), ("x", "zg"), split_axis=0, concat_axis=0, tiled=True
+        landed.reshape(16, MSG // 2, 2, 128),
+        ("zh", "x", "zg"),
+        split_axis=0,
+        concat_axis=0,
+        axis_index_groups=WINDOWS,
+        tiled=True,
     ).reshape(16 * MSG, 128)
 
     out = shape(*q.shape, dtype=BF16)
-    return pl.pallas_call(
+    q_grad, k_grad, v_grad, f_grad = pl.pallas_call(
         finish_kernel,
-        out_shape=(out, out, out, shape(*filters.shape)),
+        out_shape=(out, out, out, shape(*filters.shape[::-1])),
         in_specs=[VMEM] * 4,
         out_specs=(VMEM,) * 4,
         compiler_params=PARAMS,
     )(home, k, v, g)
+    return q_grad, k_grad, v_grad, f_grad.T
 
 
 def solution(mesh):

time: 78.2 us -> 75.1 us (0.960); the launches traced: 77.8 us -> 73.6 us
  blocking collectives: 33.8 us -> 30 us
  local copies, waits for them, and re-layouts: 1.56 us -> 0.05 us
  Pallas kernels: 3.97 us -> 5.1 us
    all_to_all x1, blocking collectives: 18.1 us -> 14.2 us  [on_device(): lax.all_to_all(landed.reshape(16, MSG // 2, 2, 128), ('zh', 'x', 'zg'), s...]
    pallas_call x1, Pallas kernels: 0.81 us -> 1.82 us  [on_device(): pl.pallas_call(pack_kernel, out_shape=shape(32 * MSG, 128), in_specs=[HBM...]
    unnamed x21 -> x18, local copies, waits for them, and re-layouts: 0.89 us -> 0.05 us
where the time goes in v2:
time: 75.1 us; the launch traced here: 73.6 us
  blocking collectives  30 us (40%)
  waiting for transfers between devices  19.1 us (25%)
  starting transfers between devices  18.6 us (25%)
  Pallas kernels  5.1 us (7%)
    all_to_all x1, waiting for transfers between devices, on_device(): lax.all_to_all(packed.reshape(32, MSG // 2, 2, 128), ('zh', 'x', 'zg'), s...  19.1 us
    all_to_all x1, starting transfers between devices, on_device(): lax.all_to_all(packed.reshape(32, MSG // 2, 2, 128), ('zh', 'x', 'zg'), s...  18.6 us
    all_to_all x1, blocking collectives, on_device(): lax.all_to_all(sent.reshape(16, 8, 128), ('zb', 'y', 'core'), split_axis=...  15.7 us
    all_to_all x1, blocking collectives, on_device(): lax.all_to_all(landed.reshape(16, MSG // 2, 2, 128), ('zh', 'x', 'zg'), s...  14.2 us
    pallas_call x1, Pallas kernels, on_device(): pl.pallas_call(pack_kernel, out_shape=shape(32 * MSG, 128), in_specs=[HBM...  1.82 us
  transfers between devices with their start and end apart: 1, of which 1 were waited for; matrix products, arithmetic and copies ran while one was open for 0% of the time, Pallas kernels for 0%

profile of v2, /device:TPU:1, one launch (start us, length us, event | category | flops | bytes accessed | tf_op | source)
XLA Modules:
  0.0 73.6 jit_solution(1250541111099946229)
XLA Ops:
  0.6 0.0 copy-start.1
  0.6 1.8 %shard_map.138 = f32[576,128]{1,0:T(8,128)} custom-call(bf16[16,1024]{1,0:T(8,128)(2,1)} %q_hbm.1, bf16[16,1024]{1,0:T(8,128)(2,1)} %k_ref.1, bf16[16,1024]{1,0:T(8,128)(2,1)} %v_ref.1, bf16[16,1024]{1,0:T(8,128)(2,1)} %g_ref.1, f32[16,256]{1,0:T(8,128)} %bitcast.15), custom_call_target="tpu_custom_call" | custom-call | tf_op jit(solution)/shard_map/pallas_call | solution.py:268
  2.5 0.0 copy-start
  2.5 0.0 copy-start.2
  2.5 0.0 copy-start.7
  2.5 18.6 %all-to-all-start = ((f32[32,9,2,128]{3,2,1,0:T(2,128)}), f32[32,9,2,128]{3,2,1,0:T(2,128)S(1)}, u32[]{:S(2)}, u32[]{:S(2)}) async-start(f32[32,9,2,128]{3,2,1,0:T(2,128)} %bitcast.14), calls=%async_computation | async-start | bytes 589824 | tf_op jit(solution)/shard_map/all_to_all | solution.py:277
  21.2 19.1 %all-to-all-done = f32[32,9,2,128]{3,2,1,0:T(2,128)S(1)} async-done(((f32[32,9,2,128]{3,2,1,0:T(2,128)}), f32[32,9,2,128]{3,2,1,0:T(2,128)S(1)}, u32[]{:S(2)}, u32[]{:S(2)}) %all-to-all-start) | async-done | bytes 294944 | tf_op jit(solution)/shard_map/all_to_all | solution.py:277
  40.3 0.0 copy-done.1
  40.3 0.0 copy-done
  40.3 0.0 copy-done.2
  40.3 0.0 copy-done.7
  40.3 0.0 copy-start.3
  40.3 1.3 %shard_map.139 = (f32[576,256]{1,0:T(8,128)S(1)}, f32[128,128]{1,0:T(8,128)S(1)}) custom-call(s32[1]{0:T(128)} %bitcast.window_ref, f32[576,128]{1,0:T(8,128)S(1)} %bitcast.9, bf16[144,192]{1,0:T(8,128)(2,1)S(1)} %copy-done.7, f32[2,72,128]{2,1,0:T(8,128)S(1)} %copy-done.2, bf16[768,256]{1,0:T(8,128)(2,1)S(1)} %copy-done, bf16[2,432,256]{2,1,0:T(8,128)(2,1)S(1)} %copy-done.1), custom_call_target="tpu_custom_call" | custom-call | tf_op jit(solution)/shard_map/pallas_call | solution.py:281
  41.6 0.0 copy-start.8
  41.6 15.7 %all_to_all.15 = f32[16,8,128]{2,1,0:T(8,128)S(1)} all-to-all(f32[16,8,128]{2,1,0:T(8,128)S(1)} %bitcast.13), channel_id=1, replica_groups=mesh['zh'=2,'x'=4,'zg'=4,'zb'=2,'y'=4,'core'=2] {'zb','y','core'}, dimensions={0} | all-to-all | bytes 131072 | tf_op jit(solution)/shard_map/all_to_all | solution.py:289
  57.3 0.0 copy-done.3
  57.3 0.0 copy-done.8
  57.3 1.2 %shard_map.140 = f32[288,128]{1,0:T(8,128)S(1)} custom-call(s32[1]{0:T(128)} %bitcast.window_ref, f32[128,128]{1,0:T(8,128)S(1)} %bitcast.12, f32[576,256]{1,0:T(8,128)S(1)} %get-tuple-element.11.spec_ref, bf16[144,768]{1,0:T(8,128)(2,1)S(1)} %copy-done.3, f32[2,72,128]{2,1,0:T(8,128)S(1)} %copy-done.2, bf16[768,256]{1,0:T(8,128)(2,1)S(1)} %copy-done, ...), custom_call_target="tpu_custom_call" | custom-call | tf_op jit(solution)/shard_map/pallas_call | solution.py:293
  58.6 0.0 copy-start.4
  58.6 0.0 copy-start.5
  58.6 0.0 copy-start.6
  58.6 14.2 %all_to_all.16 = f32[16,9,2,128]{3,2,1,0:T(2,128)S(1)} all-to-all(f32[16,9,2,128]{3,2,1,0:T(2,128)S(1)} %bitcast.11), channel_id=1, replica_groups={{0,16,288,304,64,80,352,368,128,144,416,432,192,208,480,496},{256,272,3..., dimensions={0} | all-to-all | bytes 294912 | tf_op jit(solution)/shard_map/all_to_all | solution.py:301
  72.8 0.0 copy-done.4
  72.8 0.0 copy-done.5
  72.8 0.0 copy-done.6
  72.9 0.8 %shard_map.141 = (bf16[16,1024]{1,0:T(8,128)(2,1)}, bf16[16,1024]{1,0:T(8,128)(2,1)}, bf16[16,1024]{1,0:T(8,128)(2,1)}, f32[16,256]{1,0:T(8,128)}) custom-call(f32[288,128]{1,0:T(8,128)S(1)} %bitcast.10, bf16[16,1024]{1,0:T(8,128)(2,1)S(1)} %copy-done.4, bf16[16,1024]{1,0:T(8,128)(2,1)S(1)} %copy-done.5, bf16[16,1024]{1,0:T(8,128)(2,1)S(1)} %copy-done.6), custom_call_target="tpu_custom_call" | custom-call | tf_op jit(solution)/shard_map/pallas_call | solution.py:311
Async XLA Ops:
  0.6 39.7 %copy-start.1 = (bf16[2,432,256]{2,1,0:T(8,128)(2,1)S(1)}, bf16[2,432,256]{2,1,0:T(8,128)(2,1)}, u32[]{:S(2)}) copy-start(bf16[2,432,256]{2,1,0:T(8,128)(2,1)} %constant.43.clone.lags_ref) | copy-start | bytes 1327108
  2.5 37.8 %copy-start = (bf16[768,256]{1,0:T(8,128)(2,1)S(1)}, bf16[768,256]{1,0:T(8,128)(2,1)}, u32[]{:S(2)}) copy-start(bf16[768,256]{1,0:T(8,128)(2,1)} %constant.41.clone.second_ref) | copy-start | bytes 1179652
  2.5 37.8 %copy-start.2 = (f32[2,72,128]{2,1,0:T(8,128)S(1)}, f32[2,72,128]{2,1,0:T(8,128)}, u32[]{:S(2)}) copy-start(f32[2,72,128]{2,1,0:T(8,128)} %constant.40.clone.twist_ref) | copy-start | bytes 221188
  2.5 37.8 %copy-start.7 = (bf16[144,192]{1,0:T(8,128)(2,1)S(1)}, bf16[144,192]{1,0:T(8,128)(2,1)}, u32[]{:S(2)}) copy-start(bf16[144,192]{1,0:T(8,128)(2,1)} %constant.38.clone.first_ref) | copy-start | bytes 165892
  2.5 37.8 %all-to-all-start = ((f32[32,9,2,128]{3,2,1,0:T(2,128)}), f32[32,9,2,128]{3,2,1,0:T(2,128)S(1)}, u32[]{:S(2)}, u32[]{:S(2)}) async-start(f32[32,9,2,128]{3,2,1,0:T(2,128)} %bitcast.14), calls=%async_computation | async-start | bytes 589824 | tf_op jit(solution)/shard_map/all_to_all | solution.py:277
  40.3 17.0 %copy-start.3 = (bf16[144,768]{1,0:T(8,128)(2,1)S(1)}, bf16[144,768]{1,0:T(8,128)(2,1)}, u32[]{:S(2)}) copy-start(bf16[144,768]{1,0:T(8,128)(2,1)} %constant.39.clone.taps_ref) | copy-start | bytes 663556
  41.6 15.7 %copy-start.8 = (bf16[2,32,432]{2,1,0:T(8,128)(2,1)S(1)}, bf16[2,32,432]{2,1,0:T(8,128)(2,1)}, u32[]{:S(2)}) copy-start(bf16[2,32,432]{2,1,0:T(8,128)(2,1)} %constant.42.clone.last_ref) | copy-start | bytes 165892
  58.6 14.3 %copy-start.4 = (bf16[16,1024]{1,0:T(8,128)(2,1)S(1)}, bf16[16,1024]{1,0:T(8,128)(2,1)}, u32[]{:S(2)}) copy-start(bf16[16,1024]{1,0:T(8,128)(2,1)} %k_ref.1) | copy-start | bytes 98308
  58.6 14.3 %copy-start.5 = (bf16[16,1024]{1,0:T(8,128)(2,1)S(1)}, bf16[16,1024]{1,0:T(8,128)(2,1)}, u32[]{:S(2)}) copy-start(bf16[16,1024]{1,0:T(8,128)(2,1)} %v_ref.1) | copy-start | bytes 98308
  58.6 14.3 %copy-start.6 = (bf16[16,1024]{1,0:T(8,128)(2,1)S(1)}, bf16[16,1024]{1,0:T(8,128)(2,1)}, u32[]{:S(2)}) copy-start(bf16[16,1024]{1,0:T(8,128)(2,1)} %g_ref.1) | copy-start | bytes 98308

commit v3 on v2

--- a/solution.py
+++ b/solution.py
@@ -19,6 +19,22 @@
     return window ^ (group // 2)
 
 
+WORKERS = [(x, group) for x in range(4) for group in range(4) if (x, group) not in ((0, 3), (2, 1))]
+WORKERS = [(0, 3)] + WORKERS[:7] + [(2, 1)] + WORKERS[7:]
+ORDER = [(1, r) for r in range(8, 16)] + [(0, r) for r in range(16)] + [(1, r) for r in range(8)]
+
+
+LEAD = 12
+
+
+def source_slot(half, x, group):
+    return ORDER.index((half, WORKERS.index((x, group))))
+
+
+def device_of(half, worker):
+    return half * 16 + worker[0] * 4 + worker[1]
+
+
 def split_table(table):
     high = table.astype(ml_dtypes.bfloat16)
     low = (table - high.astype(np.float64)).astype(ml_dtypes.bfloat16)
@@ -38,8 +54,9 @@
     first3 = np.concatenate([high, high, low], axis=1)
 
     taps3 = []
+    sources = np.array([device_of(half, WORKERS[r]) for half, r in ORDER])
     for parity in range(2):
-        part = np.tile(first[:, parity::2], (1, 4))
+        part = np.tile(first[:, 2 * sources + parity], (1, 4))
         high, low = split_table(part)
         taps3 += [high, high, low]
     taps3 = np.concatenate(taps3, axis=1)
@@ -61,7 +78,7 @@
         high, low = split_table(last[half * 32 : half * 32 + 32])
         last3.append(np.concatenate([high, high, low], axis=1))
     for window in range(2):
-        rows = [half_of(group, window) * 32 + x * 8 + group * 2 for x in range(4) for group in range(4)]
+        rows = [half_of(group, window) * 32 + x * 8 + group * 2 for x, group in WORKERS]
         part = np.concatenate([np.tile(last[np.array(rows) + parity].T, (1, 8)) for parity in range(2)], axis=1)
         high, low = split_table(part)
         lags3.append(np.concatenate([high, low, high], axis=0))
@@ -105,7 +122,24 @@
     return lax.broadcasted_iota(jnp.int32, (rows, 128), 1) // width
 
 
-def pack_kernel(q_hbm, k_hbm, v_hbm, g_hbm, f_hbm, out_ref, q_ref, k_ref, v_ref, g_ref, f_ref, sems):
+def put_messages(out_ref, row, values):
+    out_ref[pl.ds(8 * MSG + row, 16, stride=MSG), :] = values
+    out_ref[pl.ds(row, 8, stride=MSG), :] = values[8:]
+    out_ref[pl.ds(24 * MSG + row, 8, stride=MSG), :] = values[:8]
+
+
+def put_places(out_ref, start, values):
+    out_ref[pl.ds(start, 4, stride=8), :] = values[4:]
+    out_ref[pl.ds(start + 32, 4, stride=8), :] = values[:4]
+
+
+def get_places(in_ref, row):
+    return jnp.concatenate(
+        [in_ref[pl.ds((m ^ LEAD) * 8 + row, 4, stride=8), :] for m in range(0, 16, 4)], axis=0
+    )
+
+
+def pack_kernel(window_ref, q_hbm, k_hbm, v_hbm, g_hbm, f_hbm, out_ref, q_ref, k_ref, v_ref, g_ref, f_ref, sems):
     sources = (f_hbm, k_hbm, v_hbm, g_hbm, q_hbm)
     targets = (f_ref, k_ref, v_ref, g_ref, q_ref)
     copies = [pltpu.make_async_copy(source, target, sems.at[i]) for i, (source, target) in enumerate(zip(sources, targets))]
@@ -115,28 +149,22 @@
         copy.wait()
     gate_in = k_ref[...].astype(F32) * v_ref[...].astype(F32)
     grad_conv = g_ref[...].astype(F32) * q_ref[...].astype(F32)
-    for copy in range(2):
-        base = copy * 16 * MSG
-        for j in range(8):
-            cols = slice(j * 128, j * 128 + 128)
-            out_ref[pl.ds(base + j, 16, stride=MSG), :] = gate_in[:, cols]
-            out_ref[pl.ds(base + 8 + j, 16, stride=MSG), :] = grad_conv[:, cols]
+    for j in range(8):
+        cols = slice(j * 128, j * 128 + 128)
+        put_messages(out_ref, j, gate_in[:, cols])
+        put_messages(out_ref, 8 + j, grad_conv[:, cols])
     for high in range(2):
         flipped = f_ref[:, high * 128 : high * 128 + 128].T
         taps = jnp.concatenate([flipped[m * 16 : m * 16 + 16, :] for m in range(8)], axis=1)
-        for copy in range(2):
-            out_ref[pl.ds(copy * 16 * MSG + 16 + high, 16, stride=MSG), :] = taps
+        put_messages(out_ref, 16 + high, taps)
 
 
 def forward_kernel(window_ref, in_ref, first_ref, twist_ref, second_ref, lags_ref, spec_ref, out_ref, taps_t, lags_t):
     columns = []
     for array in range(2):
         for chan in range(4):
-            tiles = [
-                in_ref[(block * 4 + chan) * MSG + array * 8 : (block * 4 + chan) * MSG + array * 8 + 8, :]
-                for block in range(8)
-            ]
-            columns.append(jnp.concatenate(tiles, axis=0))
+            starts = [source_slot(block // 4, block % 4, chan) * MSG + array * 8 for block in range(8)]
+            columns.append(jnp.concatenate([in_ref[start : start + 8, :] for start in starts], axis=0))
     signals = jnp.concatenate(columns, axis=1)
     section = mm(first_ref[...], rows3(signals))
     stacked = []
@@ -167,17 +195,17 @@
     for high in range(2):
         taps = in_ref[pl.ds(16 + high, 32, stride=MSG), :]
         taps_t[...] = jnp.concatenate([taps] * 4, axis=0).T
-        base = high * 64
+        base = (high ^ LEAD // 8) * 64
         for b in range(4):
             row = zero
             for a in range(4):
                 row = jnp.where(group4 == a, taps_t[pl.ds(4 * a + b, 8, stride=16), :], row)
-            out_ref[pl.ds(base + b, 8, stride=8), :] = row
+            put_places(out_ref, base + b, row)
         for b in range(2):
             row = zero
             for a in range(8):
                 row = jnp.where(group8 == a, lags_t[pl.ds(high * 128 + 2 * a + b, 8, stride=16), :], row)
-            out_ref[pl.ds(base + 4 + b, 8, stride=8), :] = row
+            put_places(out_ref, base + 4 + b, row)
         for b in range(2):
             out_ref[pl.ds(base + 6 + b, 8, stride=8), :] = zero
 
@@ -186,11 +214,11 @@
     group8 = lane_group(16, 16)
     group4 = lane_group(32, 16)
     for b in range(4):
-        row = in_ref[pl.ds(b, 16, stride=8), :]
+        row = get_places(in_ref, b)
         for a in range(4):
             taps_t[pl.ds(4 * a + b, 16, stride=16), :] = jnp.where(group4 == a, row, 0.0)
     for b in range(2):
-        row = in_ref[pl.ds(4 + b, 16, stride=8), :]
+        row = get_places(in_ref, 4 + b)
         for a in range(8):
             lags_t[pl.ds(2 * a + b, 16, stride=16), :] = jnp.where(group8 == a, row, 0.0)
     for high in range(2):
@@ -227,7 +255,7 @@
         for i, s in enumerate(order):
             array, chan = s // 4, s % 4
             for block in range(4):
-                start = (block * 4 + chan) * MSG + array * 8
+                start = WORKERS.index((block, chan)) * MSG + array * 8
                 out_ref[start : start + 8, :] = landed[block * 8 : block * 8 + 8, i * 128 : i * 128 + 128]
 
 
@@ -252,9 +280,7 @@
 PARAMS = pltpu.CompilerParams(vmem_limit_bytes=32 * 1024 * 1024)
 
 
-WINDOWS = [
-    [half_of(group, window) * 16 + x * 4 + group for x in range(4) for group in range(4)] for window in range(2)
-]
+WINDOWS = [[device_of(half_of(worker[1], window), worker) for worker in WORKERS] for window in range(2)]
 
 
 def shape(*dims, dtype=F32):
@@ -268,14 +294,19 @@
     packed = pl.pallas_call(
         pack_kernel,
         out_shape=shape(32 * MSG, 128),
-        in_specs=[HBM] * 5,
+        in_specs=[SMEM] + [HBM] * 5,
         out_specs=VMEM,
         scratch_shapes=[pltpu.VMEM(q.shape, BF16)] * 4
         + [pltpu.VMEM(filters.shape[::-1], F32), pltpu.SemaphoreType.DMA((5,))],
         compiler_params=pltpu.CompilerParams(vmem_limit_bytes=60 * 1024 * 1024),
-    )(q, k, v, g, filters.T)
+    )(window, q, k, v, g, filters.T)
     arrived = lax.all_to_all(
-        packed.reshape(32, MSG // 2, 2, 128), ("zh", "x", "zg"), split_axis=0, concat_axis=0, tiled=True
+        packed.reshape(32, MSG // 2, 2, 128),
+        ("zh", "x", "zg"),
+        split_axis=0,
+        concat_axis=0,
+        axis_index_groups=[[device_of(half, WORKERS[r]) for half, r in ORDER]],
+        tiled=True,
     ).reshape(32 * MSG, 128)
 
     spec, sent = pl.pallas_call(
@@ -287,7 +318,12 @@
         compiler_params=PARAMS,
     )(window, arrived, first3, twist, second3, lags3)
     swapped = lax.all_to_all(
-        sent.reshape(16, 8, 128), ("zb", "y", "core"), split_axis=0, concat_axis=0, tiled=True
+        sent.reshape(16, 8, 128),
+        ("zb", "y", "core"),
+        split_axis=0,
+        concat_axis=0,
+        axis_index_groups=[[slot ^ LEAD for slot in range(16)]],
+        tiled=True,
     ).reshape(128, 128)
 
     landed = pl.pallas_call(

time: 75.1 us -> 68.6 us (0.913)
  the two profiles are of different devices: /device:TPU:1 before, /device:TPU:8 now
where the time goes in v3:
time: 68.6 us; the launch traced here: 68.3 us
  blocking collectives  62.4 us (91%)
  Pallas kernels  5.1 us (7%)
  between operations  0.74 us (1%)
    all_to_all x1, blocking collectives, on_device(): lax.all_to_all(packed.reshape(32, MSG // 2, 2, 128), ('zh', 'x', 'zg'), s...  34.9 us
    all_to_all x1, blocking collectives, on_device(): lax.all_to_all(landed.reshape(16, MSG // 2, 2, 128), ('zh', 'x', 'zg'), s...  18.4 us
    all_to_all x1, blocking collectives, on_device(): lax.all_to_all(sent.reshape(16, 8, 128), ('zb', 'y', 'core'), split_axis=...  9.09 us
    pallas_call x1, Pallas kernels, on_device(): pl.pallas_call(pack_kernel, out_shape=shape(32 * MSG, 128), in_specs=[SME...  1.81 us

profile of v3, /device:TPU:8, one launch (start us, length us, event | category | flops | bytes accessed | tf_op | source)
XLA Modules:
  0.0 68.3 jit_solution(2639157235961555642)
XLA Ops:
  0.6 0.0 copy-start.1
  0.7 1.8 %shard_map.138 = f32[576,128]{1,0:T(8,128)} custom-call(s32[1]{0:T(128)} %bitcast.window_ref, bf16[16,1024]{1,0:T(8,128)(2,1)} %q_hbm.1, bf16[16,1024]{1,0:T(8,128)(2,1)} %k_ref.1, bf16[16,1024]{1,0:T(8,128)(2,1)} %v_ref.1, bf16[16,1024]{1,0:T(8,128)(2,1)} %g_ref.1, f32[16,256]{1,0:T(8,128)} %bitcast.15), custom_call_target="tpu_custom_call" | custom-call | tf_op jit(solution)/shard_map/pallas_call | solution.py:294
  2.5 0.0 copy-start
  2.5 0.0 copy-start.2
  2.5 0.0 copy-start.7
  2.5 34.9 %all_to_all.15 = f32[32,9,2,128]{3,2,1,0:T(2,128)S(1)} all-to-all(f32[32,9,2,128]{3,2,1,0:T(2,128)} %bitcast.14), channel_id=1, replica_groups={{400,384,416,432,448,464,480,496,48,0,16,32,64,80,96,112,144,128,160,17..., dimensions={0} | all-to-all | bytes 589824 | tf_op jit(solution)/shard_map/all_to_all | solution.py:303
  37.4 0.0 copy-done.1
  37.4 0.0 copy-done
  37.4 0.0 copy-done.2
  37.4 0.0 copy-done.7
  37.4 0.0 copy-start.3
  37.4 1.3 %shard_map.139 = (f32[576,256]{1,0:T(8,128)S(1)}, f32[128,128]{1,0:T(8,128)S(1)}) custom-call(s32[1]{0:T(128)} %bitcast.window_ref, f32[576,128]{1,0:T(8,128)S(1)} %bitcast.9, bf16[144,192]{1,0:T(8,128)(2,1)S(1)} %copy-done.7, f32[2,72,128]{2,1,0:T(8,128)S(1)} %copy-done.2, bf16[768,256]{1,0:T(8,128)(2,1)S(1)} %copy-done, bf16[2,432,256]{2,1,0:T(8,128)(2,1)S(1)} %copy-done.1), custom_call_target="tpu_custom_call" | custom-call | tf_op jit(solution)/shard_map/pallas_call | solution.py:312
  38.7 0.0 copy-start.8
  38.7 9.1 %all_to_all.16 = f32[16,8,128]{2,1,0:T(8,128)S(1)} all-to-all(f32[16,8,128]{2,1,0:T(8,128)S(1)} %bitcast.13), channel_id=1, replica_groups={{12,13,14,15,8,9,10,11,4,5,6,7,0,1,2,3},{28,29,30,31,24,25,26,27,20,21,..., dimensions={0} | all-to-all | bytes 131072 | tf_op jit(solution)/shard_map/all_to_all | solution.py:320
  47.8 0.0 copy-done.3
  47.8 0.0 copy-done.8
  47.8 1.2 %shard_map.140 = f32[288,128]{1,0:T(8,128)S(1)} custom-call(s32[1]{0:T(128)} %bitcast.window_ref, f32[128,128]{1,0:T(8,128)S(1)} %bitcast.12, f32[576,256]{1,0:T(8,128)S(1)} %get-tuple-element.11.spec_ref, bf16[144,768]{1,0:T(8,128)(2,1)S(1)} %copy-done.3, f32[2,72,128]{2,1,0:T(8,128)S(1)} %copy-done.2, bf16[768,256]{1,0:T(8,128)(2,1)S(1)} %copy-done, ...), custom_call_target="tpu_custom_call" | custom-call | tf_op jit(solution)/shard_map/pallas_call | solution.py:329
  49.0 0.0 copy-start.4
  49.0 0.0 copy-start.5
  49.0 0.0 copy-start.6
  49.0 18.4 %all_to_all.17 = f32[16,9,2,128]{3,2,1,0:T(2,128)S(1)} all-to-all(f32[16,9,2,128]{3,2,1,0:T(2,128)S(1)} %bitcast.11), channel_id=1, replica_groups={{304,0,16,288,64,80,352,368,144,128,416,432,192,208,480,496},{48,256,27..., dimensions={0} | all-to-all | bytes 294912 | tf_op jit(solution)/shard_map/all_to_all | solution.py:337
  67.5 0.0 copy-done.4
  67.5 0.0 copy-done.5
  67.5 0.0 copy-done.6
  67.5 0.8 %shard_map.141 = (bf16[16,1024]{1,0:T(8,128)(2,1)}, bf16[16,1024]{1,0:T(8,128)(2,1)}, bf16[16,1024]{1,0:T(8,128)(2,1)}, f32[16,256]{1,0:T(8,128)}) custom-call(f32[288,128]{1,0:T(8,128)S(1)} %bitcast.10, bf16[16,1024]{1,0:T(8,128)(2,1)S(1)} %copy-done.4, bf16[16,1024]{1,0:T(8,128)(2,1)S(1)} %copy-done.5, bf16[16,1024]{1,0:T(8,128)(2,1)S(1)} %copy-done.6), custom_call_target="tpu_custom_call" | custom-call | tf_op jit(solution)/shard_map/pallas_call | solution.py:347
Async XLA Ops:
  0.6 36.7 %copy-start.1 = (bf16[2,432,256]{2,1,0:T(8,128)(2,1)S(1)}, bf16[2,432,256]{2,1,0:T(8,128)(2,1)}, u32[]{:S(2)}) copy-start(bf16[2,432,256]{2,1,0:T(8,128)(2,1)} %constant.43.clone.lags_ref) | copy-start | bytes 1327108
  2.5 34.9 %copy-start = (bf16[768,256]{1,0:T(8,128)(2,1)S(1)}, bf16[768,256]{1,0:T(8,128)(2,1)}, u32[]{:S(2)}) copy-start(bf16[768,256]{1,0:T(8,128)(2,1)} %constant.41.clone.second_ref) | copy-start | bytes 1179652
  2.5 34.9 %copy-start.2 = (f32[2,72,128]{2,1,0:T(8,128)S(1)}, f32[2,72,128]{2,1,0:T(8,128)}, u32[]{:S(2)}) copy-start(f32[2,72,128]{2,1,0:T(8,128)} %constant.40.clone.twist_ref) | copy-start | bytes 221188
  2.5 34.9 %copy-start.7 = (bf16[144,192]{1,0:T(8,128)(2,1)S(1)}, bf16[144,192]{1,0:T(8,128)(2,1)}, u32[]{:S(2)}) copy-start(bf16[144,192]{1,0:T(8,128)(2,1)} %constant.38.clone.first_ref) | copy-start | bytes 165892
  37.4 10.4 %copy-start.3 = (bf16[144,768]{1,0:T(8,128)(2,1)S(1)}, bf16[144,768]{1,0:T(8,128)(2,1)}, u32[]{:S(2)}) copy-start(bf16[144,768]{1,0:T(8,128)(2,1)} %constant.39.clone.taps_ref) | copy-start | bytes 663556
  38.7 9.1 %copy-start.8 = (bf16[2,32,432]{2,1,0:T(8,128)(2,1)S(1)}, bf16[2,32,432]{2,1,0:T(8,128)(2,1)}, u32[]{:S(2)}) copy-start(bf16[2,32,432]{2,1,0:T(8,128)(2,1)} %constant.42.clone.last_ref) | copy-start | bytes 165892
  49.0 18.5 %copy-start.4 = (bf16[16,1024]{1,0:T(8,128)(2,1)S(1)}, bf16[16,1024]{1,0:T(8,128)(2,1)}, u32[]{:S(2)}) copy-start(bf16[16,1024]{1,0:T(8,128)(2,1)} %k_ref.1) | copy-start | bytes 98308
  49.0 18.5 %copy-start.5 = (bf16[16,1024]{1,0:T(8,128)(2,1)S(1)}, bf16[16,1024]{1,0:T(8,128)(2,1)}, u32[]{:S(2)}) copy-start(bf16[16,1024]{1,0:T(8,128)(2,1)} %v_ref.1) | copy-start | bytes 98308
  49.0 18.5 %copy-start.6 = (bf16[16,1024]{1,0:T(8,128)(2,1)S(1)}, bf16[16,1024]{1,0:T(8,128)(2,1)}, u32[]{:S(2)}) copy-start(bf16[16,1024]{1,0:T(8,128)(2,1)} %g_ref.1) | copy-start | bytes 98308

commit v4 on v3

--- a/solution.py
+++ b/solution.py
@@ -139,14 +139,7 @@
     )
 
 
-def pack_kernel(window_ref, q_hbm, k_hbm, v_hbm, g_hbm, f_hbm, out_ref, q_ref, k_ref, v_ref, g_ref, f_ref, sems):
-    sources = (f_hbm, k_hbm, v_hbm, g_hbm, q_hbm)
-    targets = (f_ref, k_ref, v_ref, g_ref, q_ref)
-    copies = [pltpu.make_async_copy(source, target, sems.at[i]) for i, (source, target) in enumerate(zip(sources, targets))]
-    for copy in copies:
-        copy.start()
-    for copy in copies:
-        copy.wait()
+def pack_kernel(place_ref, q_ref, k_ref, v_ref, g_ref, f_ref, out_ref):
     gate_in = k_ref[...].astype(F32) * v_ref[...].astype(F32)
     grad_conv = g_ref[...].astype(F32) * q_ref[...].astype(F32)
     for j in range(8):
@@ -275,7 +268,6 @@
 
 
 SMEM = pl.BlockSpec(memory_space=pltpu.SMEM)
-HBM = pl.BlockSpec(memory_space=pltpu.HBM)
 VMEM = pl.BlockSpec(memory_space=pltpu.VMEM)
 PARAMS = pltpu.CompilerParams(vmem_limit_bytes=32 * 1024 * 1024)
 
@@ -291,15 +283,14 @@
     first3, taps3, twist, second3, last3, lags3 = (jnp.asarray(t) for t in tables())
     window = (lax.axis_index("zh") ^ (lax.axis_index("zg") // 2)).astype(jnp.int32).reshape(1)
 
+    place = jnp.broadcast_to(window.astype(F32), (512, 128))
     packed = pl.pallas_call(
         pack_kernel,
         out_shape=shape(32 * MSG, 128),
-        in_specs=[SMEM] + [HBM] * 5,
+        in_specs=[VMEM] * 6,
         out_specs=VMEM,
-        scratch_shapes=[pltpu.VMEM(q.shape, BF16)] * 4
-        + [pltpu.VMEM(filters.shape[::-1], F32), pltpu.SemaphoreType.DMA((5,))],
-        compiler_params=pltpu.CompilerParams(vmem_limit_bytes=60 * 1024 * 1024),
-    )(window, q, k, v, g, filters.T)
+        compiler_params=PARAMS,
+    )(place, q, k, v, g, filters.T)
     arrived = lax.all_to_all(
         packed.reshape(32, MSG // 2, 2, 128),
         ("zh", "x", "zg"),
@@ -312,7 +303,7 @@
     spec, sent = pl.pallas_call(
         forward_kernel,
         out_shape=(shape(8 * ROWS, 256), shape(128, 128)),
-        in_specs=[SMEM] + [VMEM] * 5,
+        in_specs=[VMEM] * 6,
         out_specs=(VMEM, VMEM),
         scratch_shapes=[pltpu.VMEM((128, 128), F32), pltpu.VMEM((256, 128), F32)],
         compiler_params=PARAMS,

time: 68.6 us -> 67.4 us (0.983)
  Pallas kernels: 5.1 us -> 3.47 us
  local copies, waits for them, and re-layouts: 0.05 us -> 0.8 us
    pallas_call x1, Pallas kernels: 1.81 us -> 0.17 us  [on_device(): pl.pallas_call(pack_kernel, out_shape=shape(32 * MSG, 128), in_specs=[VME...]
    unnamed x18 -> x22, local copies, waits for them, and re-layouts: 0.05 us -> 0.78 us
where the time goes in v4:
time: 67.4 us; the launch traced here: 67.1 us
  blocking collectives  62 us (92%)
  Pallas kernels  3.47 us (5%)
  local copies, waits for them, and re-layouts  0.8 us (1%)
  between operations  0.76 us (1%)
    all_to_all x1, blocking collectives, on_device(): lax.all_to_all(packed.reshape(32, MSG // 2, 2, 128), ('zh', 'x', 'zg'), s...  34.6 us
    all_to_all x1, blocking collectives, on_device(): lax.all_to_all(landed.reshape(16, MSG // 2, 2, 128), ('zh', 'x', 'zg'), s...  18.3 us
    all_to_all x1, blocking collectives, on_device(): lax.all_to_all(sent.reshape(16, 8, 128), ('zb', 'y', 'core'), split_axis=...  9.08 us

profile of v4, /device:TPU:8, one launch (start us, length us, event | category | flops | bytes accessed | tf_op | source)
XLA Modules:
  0.0 67.1 jit_solution(14947016409173796030)
XLA Ops:
  0.6 0.0 copy-start.4
  0.7 0.0 copy-start.5
  0.7 0.0 copy-start.6
  0.7 0.0 copy-start.9
  0.7 0.0 copy-start.10
  0.7 0.7 %copy-done.4 = bf16[16,1024]{1,0:T(8,128)(2,1)S(1)} copy-done((bf16[16,1024]{1,0:T(8,128)(2,1)S(1)}, bf16[16,1024]{1,0:T(8,128)(2,1)}, u32[]{:S(2)}) %copy-start.4) | copy-done | bytes 32792
  1.4 0.0 copy-done.5
  1.4 0.0 copy-done.6
  1.4 0.0 copy-done.9
  1.5 0.0 copy-done.10
  1.5 0.0 copy-start.1
  1.5 0.2 shard_map.138
  1.6 0.0 copy-start
  1.7 0.0 copy-start.2
  1.7 0.0 copy-start.7
  1.7 34.6 %all_to_all.15 = f32[32,9,2,128]{3,2,1,0:T(2,128)S(1)} all-to-all(f32[32,9,2,128]{3,2,1,0:T(2,128)S(1)} %bitcast.11), channel_id=1, replica_groups={{400,384,416,432,448,464,480,496,48,0,16,32,64,80,96,112,144,128,160,17..., dimensions={0} | all-to-all | bytes 589824 | tf_op jit(solution)/shard_map/all_to_all | solution.py:294
  36.3 0.0 copy-done.1
  36.3 0.0 copy-done
  36.3 0.0 copy-done.2
  36.3 0.0 copy-done.7
  36.3 0.0 copy-start.3
  36.4 1.3 %shard_map.139 = (f32[576,256]{1,0:T(8,128)S(1)}, f32[128,128]{1,0:T(8,128)S(1)}) custom-call(s32[1]{0:T(128)} %bitcast.window_ref, f32[576,128]{1,0:T(8,128)S(1)} %bitcast.10, bf16[144,192]{1,0:T(8,128)(2,1)S(1)} %copy-done.7, f32[2,72,128]{2,1,0:T(8,128)S(1)} %copy-done.2, bf16[768,256]{1,0:T(8,128)(2,1)S(1)} %copy-done, bf16[2,432,256]{2,1,0:T(8,128)(2,1)S(1)} %copy-done.1), custom_call_target="tpu_custom_call" | custom-call | tf_op jit(solution)/shard_map/pallas_call | solution.py:303
  37.6 0.0 copy-start.8
  37.6 9.1 %all_to_all.16 = f32[16,8,128]{2,1,0:T(8,128)S(1)} all-to-all(f32[16,8,128]{2,1,0:T(8,128)S(1)} %bitcast.15), channel_id=1, replica_groups={{12,13,14,15,8,9,10,11,4,5,6,7,0,1,2,3},{28,29,30,31,24,25,26,27,20,21,..., dimensions={0} | all-to-all | bytes 131072 | tf_op jit(solution)/shard_map/all_to_all | solution.py:311
  46.7 0.0 copy-done.3
  46.7 0.0 copy-done.8
  46.7 1.2 %shard_map.140 = f32[288,128]{1,0:T(8,128)S(1)} custom-call(s32[1]{0:T(128)} %bitcast.window_ref, f32[128,128]{1,0:T(8,128)S(1)} %bitcast.14, f32[576,256]{1,0:T(8,128)S(1)} %get-tuple-element.11.spec_ref, bf16[144,768]{1,0:T(8,128)(2,1)S(1)} %copy-done.3, f32[2,72,128]{2,1,0:T(8,128)S(1)} %copy-done.2, bf16[768,256]{1,0:T(8,128)(2,1)S(1)} %copy-done, ...), custom_call_target="tpu_custom_call" | custom-call | tf_op jit(solution)/shard_map/pallas_call | solution.py:320
  48.0 18.3 %all_to_all.17 = f32[16,9,2,128]{3,2,1,0:T(2,128)S(1)} all-to-all(f32[16,9,2,128]{3,2,1,0:T(2,128)S(1)} %bitcast.13), channel_id=1, replica_groups={{304,0,16,288,64,80,352,368,144,128,416,432,192,208,480,496},{48,256,27..., dimensions={0} | all-to-all | bytes 294912 | tf_op jit(solution)/shard_map/all_to_all | solution.py:328
  66.3 0.8 %shard_map.141 = (bf16[16,1024]{1,0:T(8,128)(2,1)}, bf16[16,1024]{1,0:T(8,128)(2,1)}, bf16[16,1024]{1,0:T(8,128)(2,1)}, f32[16,256]{1,0:T(8,128)}) custom-call(f32[288,128]{1,0:T(8,128)S(1)} %bitcast.12, bf16[16,1024]{1,0:T(8,128)(2,1)S(1)} %copy-done.4, bf16[16,1024]{1,0:T(8,128)(2,1)S(1)} %copy-done.5, bf16[16,1024]{1,0:T(8,128)(2,1)S(1)} %copy-done.6), custom_call_target="tpu_custom_call" | custom-call | tf_op jit(solution)/shard_map/pallas_call | solution.py:338
  (1 shorter events, 0.0 us)
Async XLA Ops:
  0.6 0.8 %copy-start.4 = (bf16[16,1024]{1,0:T(8,128)(2,1)S(1)}, bf16[16,1024]{1,0:T(8,128)(2,1)}, u32[]{:S(2)}) copy-start(bf16[16,1024]{1,0:T(8,128)(2,1)} %k_ref.3) | copy-start | bytes 98308
  0.7 0.8 %copy-start.5 = (bf16[16,1024]{1,0:T(8,128)(2,1)S(1)}, bf16[16,1024]{1,0:T(8,128)(2,1)}, u32[]{:S(2)}) copy-start(bf16[16,1024]{1,0:T(8,128)(2,1)} %v_ref.3) | copy-start | bytes 98308
  0.7 0.8 %copy-start.6 = (bf16[16,1024]{1,0:T(8,128)(2,1)S(1)}, bf16[16,1024]{1,0:T(8,128)(2,1)}, u32[]{:S(2)}) copy-start(bf16[16,1024]{1,0:T(8,128)(2,1)} %g_ref.3) | copy-start | bytes 98308
  0.7 0.8 %copy-start.9 = (bf16[16,1024]{1,0:T(8,128)(2,1)S(1)}, bf16[16,1024]{1,0:T(8,128)(2,1)}, u32[]{:S(2)}) copy-start(bf16[16,1024]{1,0:T(8,128)(2,1)} %q_ref.1) | copy-start | bytes 98308
  0.7 0.8 %copy-start.10 = (f32[256,16]{0,1:T(8,128)S(1)}, f32[256,16]{0,1:T(8,128)}, u32[]{:S(2)}) copy-start(f32[256,16]{0,1:T(8,128)} %param.14) | copy-start | bytes 49156
  1.5 34.9 %copy-start.1 = (bf16[2,432,256]{2,1,0:T(8,128)(2,1)S(1)}, bf16[2,432,256]{2,1,0:T(8,128)(2,1)}, u32[]{:S(2)}) copy-start(bf16[2,432,256]{2,1,0:T(8,128)(2,1)} %constant.43.clone.lags_ref) | copy-start | bytes 1327108
  1.6 34.7 %copy-start = (bf16[768,256]{1,0:T(8,128)(2,1)S(1)}, bf16[768,256]{1,0:T(8,128)(2,1)}, u32[]{:S(2)}) copy-start(bf16[768,256]{1,0:T(8,128)(2,1)} %constant.41.clone.second_ref) | copy-start | bytes 1179652
  1.7 34.7 %copy-start.2 = (f32[2,72,128]{2,1,0:T(8,128)S(1)}, f32[2,72,128]{2,1,0:T(8,128)}, u32[]{:S(2)}) copy-start(f32[2,72,128]{2,1,0:T(8,128)} %constant.40.clone.twist_ref) | copy-start | bytes 221188
  1.7 34.7 %copy-start.7 = (bf16[144,192]{1,0:T(8,128)(2,1)S(1)}, bf16[144,192]{1,0:T(8,128)(2,1)}, u32[]{:S(2)}) copy-start(bf16[144,192]{1,0:T(8,128)(2,1)} %constant.38.clone.first_ref) | copy-start | bytes 165892
  36.3 10.4 %copy-start.3 = (bf16[144,768]{1,0:T(8,128)(2,1)S(1)}, bf16[144,768]{1,0:T(8,128)(2,1)}, u32[]{:S(2)}) copy-start(bf16[144,768]{1,0:T(8,128)(2,1)} %constant.39.clone.taps_ref) | copy-start | bytes 663556
  37.6 9.1 %copy-start.8 = (bf16[2,32,432]{2,1,0:T(8,128)(2,1)S(1)}, bf16[2,32,432]{2,1,0:T(8,128)(2,1)}, u32[]{:S(2)}) copy-start(bf16[2,32,432]{2,1,0:T(8,128)(2,1)} %constant.42.clone.last_ref) | copy-start | bytes 165892

commit v5 on v4

v5 whole, which is shorter than its diff:
```python
import ml_dtypes
import numpy as np
import jax
import jax.numpy as jnp
from jax import lax
from jax.experimental import pallas as pl
from jax.experimental.pallas import tpu as pltpu
from jax.sharding import Mesh
from jax.sharding import PartitionSpec as P

N = 16384
ROWS = 72
F32 = jnp.float32
BF16 = jnp.bfloat16
MSG = 18


LEAD = 12
LEAD_PLACE = 12


def split_table(table):
    high = table.astype(ml_dtypes.bfloat16)
    low = (table - high.astype(np.float64)).astype(ml_dtypes.bfloat16)
    return high, low


def tables():
    k1 = np.arange(ROWS)
    live = (k1 <= 64).astype(np.float64)
    t1 = np.arange(64)
    t2 = np.arange(128)
    turn = 2 * np.pi / 128

    angle = turn * (k1[:, None] * t1[None, :] % 128)
    first = np.concatenate([live[:, None] * np.cos(angle), -live[:, None] * np.sin(angle)])
    high, low = split_table(first)
    first3 = np.concatenate([high, high, low], axis=1)

    sources = np.arange(16) ^ LEAD
    taps3 = []
    for part in range(4):
        high, low = split_table(np.tile(first[:, 4 * sources + part], (1, 8)))
        taps3 += [high, high, low]
    taps3 = np.concatenate(taps3, axis=1)

    angle = 2 * np.pi / N * (k1[:, None] * t2[None, :] % N)
    twist = np.stack([live[:, None] * np.cos(angle), live[:, None] * np.sin(angle)]).astype(np.float32)

    angle = turn * (t2[:, None] * t2[None, :] % 128)
    cos, sin = np.cos(angle), np.sin(angle)
    second = np.block([[cos, -sin], [sin, cos]])
    high, low = split_table(second)
    second3 = np.concatenate([high, low, high], axis=0)

    weight = live * np.where((k1 == 0) | (k1 == 64), 1.0, 2.0) / N
    angle = turn * (t1[:, None] * k1[None, :] % 128)
    last = np.concatenate([weight * np.cos(angle), weight * np.sin(angle)], axis=1)
    high, low = split_table(last)
    last3 = np.concatenate([high, high, low], axis=1)
    lags = np.concatenate([np.tile(last[4 * sources + part].T, (1, 8)) for part in range(4)], axis=1)
    high, low = split_table(lags)
    lags3 = np.concatenate([high, low, high], axis=0)
    return first3, taps3, twist, second3, last3, lags3


def halves(x):
    high = x.astype(BF16)
    return high, (x - high.astype(F32)).astype(BF16)


def lanes3(x):
    high, low = halves(x)
    return jnp.concatenate([high, low, high], axis=1)


def lanes3_table_last(x):
    high, low = halves(x)
    return jnp.concatenate([high, high, low], axis=1)


def rows3(x):
    high, low = halves(x)
    return jnp.concatenate([high, low, high], axis=0)


def mm(a, b):
    return jnp.dot(a, b, preferred_element_type=F32)


def turned(x_re, x_im, twist_ref):
    cos, sin = twist_ref[0], twist_ref[1]
    return x_re * cos + x_im * sin, x_im * cos - x_re * sin


def second_stage(stacked, second_ref):
    return mm(lanes3_table_last(stacked), second_ref[...])


def lane_group(width, rows):
    return lax.broadcasted_iota(jnp.int32, (rows, 128), 1) // width


def put_places(out_ref, part, row, values):
    start = (part * 8 ^ LEAD_PLACE & 24) * 4 + row
    out_ref[pl.ds(start, 4, stride=4), :] = values[4:]
    out_ref[pl.ds(start + 16, 4, stride=4), :] = values[:4]


def get_places(in_ref, low, row):
    return jnp.concatenate(
        [in_ref[pl.ds((low * 16 + m ^ LEAD_PLACE) * 4 + row, 4, stride=4), :] for m in range(0, 16, 4)], axis=0
    )


def pack_kernel(place_ref, q_ref, k_ref, v_ref, g_ref, f_ref, out_ref):
    gate_in = k_ref[...].astype(F32) * v_ref[...].astype(F32)
    grad_conv = g_ref[...].astype(F32) * q_ref[...].astype(F32)
    for j in range(8):
        cols = slice(j * 128, j * 128 + 128)
        out_ref[pl.ds(j, 16, stride=MSG), :] = gate_in[:, cols]
        out_ref[pl.ds(8 + j, 16, stride=MSG), :] = grad_conv[:, cols]
    for high in range(2):
        flipped = f_ref[:, high * 128 : high * 128 + 128].T
        taps = jnp.concatenate([flipped[m * 16 : m * 16 + 16, :] for m in range(8)], axis=1)
        out_ref[pl.ds(16 + high, 16, stride=MSG), :] = taps


def message_start(block, chan, array):
    return (block * 2 + chan ^ LEAD) * MSG + array * 8


def forward_kernel(in_ref, first_ref, twist_ref, second_ref, lags_ref, spec_ref, out_ref, taps_t, lags_t):
    columns = []
    for array in range(2):
        for chan in range(2):
            starts = [message_start(block, chan, array) for block in range(8)]
            columns.append(jnp.concatenate([in_ref[start : start + 8, :] for start in starts], axis=0))
    signals = jnp.concatenate(columns, axis=1)
    section = mm(first_ref[...], rows3(signals))
    stacked = []
    for s in range(4):
        cols = slice(s * 128, s * 128 + 128)
        re, im = turned(section[:ROWS, cols], section[ROWS:, cols], twist_ref)
        stacked.append(jnp.concatenate([re, im], axis=1))
    spec = second_stage(jnp.concatenate(stacked, axis=0), second_ref)
    spec_ref[...] = spec

    sum_re = jnp.zeros((ROWS, 128), F32)
    sum_im = jnp.zeros((ROWS, 128), F32)
    for chan in range(2):
        x = spec[chan * ROWS : chan * ROWS + ROWS]
        g = spec[(2 + chan) * ROWS : (2 + chan) * ROWS + ROWS]
        sum_re += g[:, :128] * x[:, :128] + g[:, 128:] * x[:, 128:]
        sum_im += g[:, :128] * x[:, 128:] - g[:, 128:] * x[:, :128]
    back = second_stage(jnp.concatenate([sum_re, sum_im], axis=1), second_ref)
    re, im = turned(back[:, :128], back[:, 128:], twist_ref)
    flipped = jnp.concatenate([re, im], axis=0).T
    lags = mm(lanes3_table_last(flipped), lags_ref[...]) * np.float32(1.0 / np.sqrt(32768.0))
    for part in range(4):
        lags_t[part * 128 : part * 128 + 128, :] = lags[:, part * 128 : part * 128 + 128]

    group = lane_group(16, 8)
    zero = jnp.zeros((8, 128), F32)
    for high in range(2):
        taps = in_ref[pl.ds(16 + high, 16, stride=MSG), :]
        taps_t[...] = jnp.concatenate([taps] * 8, axis=0).T
        for b in range(2):
            row = zero
            for a in range(8):
                row = jnp.where(group == a, taps_t[pl.ds(2 * a + b, 8, stride=16), :], row)
            for low in range(2):
                put_places(out_ref, low * 2 + high, b, row)
    for part in range(4):
        for b in range(2):
            row = zero
            for a in range(8):
                row = jnp.where(group == a, lags_t[pl.ds(part * 128 + 2 * a + b, 8, stride=16), :], row)
            put_places(out_ref, part, 2 + b, row)


def backward_kernel(in_ref, spec_ref, taps_ref, twist_ref, second_ref, last_ref, out_ref, taps_t, lags_t):
    group = lane_group(16, 16)
    for b in range(2):
        for low in range(2):
            row = get_places(in_ref, low, b)
            for a in range(8):
                taps_t[pl.ds(low * 256 + 2 * a + b, 16, stride=16), :] = jnp.where(group == a, row, 0.0)
        row = get_places(in_ref, 0, 2 + b) + get_places(in_ref, 1, 2 + b)
        for a in range(8):
            lags_t[pl.ds(2 * a + b, 16, stride=16), :] = jnp.where(group == a, row, 0.0)
    for high in range(2):
        flipped = lags_t[high * 128 : high * 128 + 128, :].T
        total = flipped[:16]
        for a in range(1, 8):
            total += flipped[a * 16 : a * 16 + 16]
        out_ref[pl.ds(16 + high, 16, stride=MSG), :] = total

    taps = jnp.concatenate([lanes3(taps_t[part * 128 : part * 128 + 128, :]) for part in range(4)], axis=1)
    section = lax.dot_general(
        taps_ref[...], taps, (((1,), (1,)), ((), ())), preferred_element_type=F32
    )
    re, im = turned(section[:ROWS], section[ROWS:], twist_ref)
    filt = second_stage(jnp.concatenate([re, im], axis=1), second_ref)
    h_re, h_im = filt[:, :128], filt[:, 128:]

    products = []
    for s in range(4):
        re, im = spec_ref[s * ROWS : s * ROWS + ROWS, :128], spec_ref[s * ROWS : s * ROWS + ROWS, 128:]
        if s < 2:
            products.append(jnp.concatenate([re * h_re - im * h_im, -(re * h_im + im * h_re)], axis=1))
        else:
            products.append(jnp.concatenate([re * h_re + im * h_im, re * h_im - im * h_re], axis=1))
    back = second_stage(jnp.concatenate(products, axis=0), second_ref)
    columns = []
    for s in range(4):
        part = back[s * ROWS : s * ROWS + ROWS]
        re, im = turned(part[:, :128], part[:, 128:], twist_ref)
        columns.append(jnp.concatenate([re, im], axis=0))
    landed = mm(last_ref[...], rows3(jnp.concatenate(columns, axis=1)))
    for s in range(4):
        array, chan = s // 2, s % 2
        for block in range(8):
            start = message_start(block, chan, array)
            out_ref[start : start + 8, :] = landed[block * 8 : block * 8 + 8, s * 128 : s * 128 + 128]


def finish_kernel(in_ref, k_ref, v_ref, g_ref, q_out, k_out, v_out, f_out):
    for j in range(8):
        cols = slice(j * 128, j * 128 + 128)
        conv = in_ref[pl.ds(j, 16, stride=MSG), :]
        grad = in_ref[pl.ds(8 + j, 16, stride=MSG), :]
        q_out[:, cols] = (g_ref[:, cols].astype(F32) * conv).astype(BF16)
        k_out[:, cols] = (grad * v_ref[:, cols].astype(F32)).astype(BF16)
        v_out[:, cols] = (grad * k_ref[:, cols].astype(F32)).astype(BF16)
    for high in range(2):
        flipped = in_ref[pl.ds(16 + high, 16, stride=MSG), :].T
        f_out[:, high * 128 : high * 128 + 128] = jnp.concatenate(
            [flipped[m * 16 : m * 16 + 16, :] for m in range(8)], axis=1
        )


VMEM = pl.BlockSpec(memory_space=pltpu.VMEM)
PARAMS = pltpu.CompilerParams(vmem_limit_bytes=32 * 1024 * 1024)


def shape(*dims, dtype=F32):
    return jax.ShapeDtypeStruct(dims, dtype)


def exchange(rows, axes, count, lead):
    messages = rows.reshape(count, rows.shape[0] // count // 2, 2, 128)
    slots = [slot ^ lead for slot in range(count)]
    arrived = lax.all_to_all(messages, axes, split_axis=0, concat_axis=0, axis_index_groups=[slots], tiled=True)
    return arrived.reshape(rows.shape)


def on_device(q, k, v, filters, g):
    first3, taps3, twist, second3, last3, lags3 = (jnp.asarray(t) for t in tables())
    place = jnp.broadcast_to(lax.axis_index("x").astype(F32), (2048, 128))
    packed = pl.pallas_call(
        pack_kernel,
        out_shape=shape(16 * MSG, 128),
        in_specs=[VMEM] * 6,
        out_specs=VMEM,
        compiler_params=PARAMS,
    )(place, q, k, v, g, filters.T)
    arrived = exchange(packed, ("zh", "x", "zgh"), 16, LEAD)

    spec, sent = pl.pallas_call(
        forward_kernel,
        out_shape=(shape(4 * ROWS, 256), shape(128, 128)),
        in_specs=[VMEM] * 5,
        out_specs=(VMEM, VMEM),
        scratch_shapes=[pltpu.VMEM((128, 128), F32), pltpu.VMEM((512, 128), F32)],
        compiler_params=PARAMS,
    )(arrived, first3, twist, second3, lags3)
    swapped = exchange(sent, ("zgl", "zb", "y", "core"), 32, LEAD_PLACE)

    landed = pl.pallas_call(
        backward_kernel,
        out_shape=shape(16 * MSG, 128),
        in_specs=[VMEM] * 6,
        out_specs=VMEM,
        scratch_shapes=[pltpu.VMEM((512, 128), F32), pltpu.VMEM((256, 128), F32)],
        compiler_params=PARAMS,
    )(swapped, spec, taps3, twist, second3, last3)
    home = exchange(landed, ("zh", "x", "zgh"), 16, LEAD)

    out = shape(*q.shape, dtype=BF16)
    q_grad, k_grad, v_grad, f_grad = pl.pallas_call(
        finish_kernel,
        out_shape=(out, out, out, shape(*filters.shape[::-1])),
        in_specs=[VMEM] * 4,
        out_specs=(VMEM,) * 4,
        compiler_params=PARAMS,
    )(home, k, v, g)
    return q_grad, k_grad, v_grad, f_grad.T


def solution(mesh):
    fine = Mesh(mesh.devices.reshape(2, 4, 2, 2, 2, 4, 2), ("zh", "x", "zgh", "zgl", "zb", "y", "core"))
    seq, chan = ("zh", "x"), ("zgh", "zgl", "zb", "y", "core")
    gates, taps = P(chan, seq), P(None, seq + chan)
    return jax.shard_map(
        on_device,
        mesh=fine,
        in_specs=(gates, gates, gates, taps, gates),
        out_specs=(gates, gates, gates, taps),
        check_vma=False,
    )
```

time: 67.4 us -> 65.3 us (0.969)
  the two profiles are of different devices: /device:TPU:8 before, /device:TPU:1 now
where the time goes in v5:
time: 65.3 us; the launch traced here: 64.9 us
  blocking collectives  60.1 us (92%)
  Pallas kernels  3.35 us (5%)
  local copies, waits for them, and re-layouts  0.8 us (1%)
  between operations  0.75 us (1%)
    all_to_all x3, blocking collectives, exchange(): lax.all_to_all(messages, axes, split_axis=0, concat_axis=0, axis_index_gr...  60.1 us

profile of v5, /device:TPU:1, one launch (start us, length us, event | category | flops | bytes accessed | tf_op | source)
XLA Modules:
  0.0 64.9 jit_solution(11942842300051134019)
XLA Ops:
  0.6 0.0 copy-start.4
  0.6 0.0 copy-start.5
  0.7 0.0 copy-start.6
  0.7 0.0 copy-start.9
  0.7 0.0 copy-start.10
  0.7 0.1 broadcast_in_dim.3.place_ref
  0.8 0.6 copy-done.4
  1.4 0.0 copy-done.5
  1.4 0.0 copy-done.6
  1.4 0.0 copy-done.9
  1.4 0.0 copy-done.10
  1.5 0.0 copy-start
  1.5 0.0 copy-start.2
  1.5 0.2 shard_map.138
  1.6 0.0 copy-start.3
  1.6 0.0 copy-start.7
  1.7 26.1 %all_to_all.15 = f32[16,9,2,128]{3,2,1,0:T(2,128)S(1)} all-to-all(f32[16,9,2,128]{3,2,1,0:T(2,128)S(1)} %bitcast.11), channel_id=1, replica_groups={{384,416,448,480,256,288,320,352,128,160,192,224,0,32,64,96},{385,417,4..., dimensions={0} | all-to-all | bytes 294912 | tf_op jit(solution)/shard_map/all_to_all | solution.py:254
  27.8 0.0 copy-done
  27.8 0.0 copy-done.2
  27.8 0.0 copy-done.3
  27.8 0.0 copy-done.7
  27.8 0.0 copy-start.1
  27.8 1.2 %shard_map.139 = (f32[288,256]{1,0:T(8,128)S(1)}, f32[128,128]{1,0:T(8,128)S(1)}) custom-call(f32[288,128]{1,0:T(8,128)S(1)} %bitcast.9, bf16[144,192]{1,0:T(8,128)(2,1)S(1)} %copy-done.7, f32[2,72,128]{2,1,0:T(8,128)S(1)} %copy-done.3, bf16[768,256]{1,0:T(8,128)(2,1)S(1)} %copy-done, bf16[432,512]{1,0:T(8,128)(2,1)S(1)} %copy-done.2), custom_call_target="tpu_custom_call" | custom-call | tf_op jit(solution)/shard_map/pallas_call | solution.py:270
  29.0 0.0 copy-start.8
  29.0 14.1 %all_to_all.16 = f32[32,2,2,128]{3,2,1,0:T(2,128)S(1)} all-to-all(f32[32,2,2,128]{3,2,1,0:T(2,128)S(1)} %bitcast.13), channel_id=1, replica_groups={{12,13,14,15,8,9,10,11,4,5,6,7,0,1,2,3,28,29,30,31,24,25,26,27,20,21,22..., dimensions={0} | all-to-all | bytes 131072 | tf_op jit(solution)/shard_map/all_to_all | solution.py:254
  43.1 0.0 copy-done.1
  43.1 0.0 copy-done.8
  43.2 1.2 %shard_map.140 = f32[288,128]{1,0:T(8,128)S(1)} custom-call(f32[128,128]{1,0:T(8,128)S(1)} %bitcast.12, f32[288,256]{1,0:T(8,128)S(1)} %get-tuple-element.11.spec_ref, bf16[144,1536]{1,0:T(8,128)(2,1)S(1)} %copy-done.1, f32[2,72,128]{2,1,0:T(8,128)S(1)} %copy-done.3, bf16[768,256]{1,0:T(8,128)(2,1)S(1)} %copy-done, bf16[64,432]{1,0:T(8,128)(2,1)S(1)} %copy-done.8), custom_call_target="tpu_custom_call" | custom-call | tf_op jit(solution)/shard_map/pallas_call | solution.py:280
  44.3 19.8 %all_to_all.17 = f32[16,9,2,128]{3,2,1,0:T(2,128)S(1)} all-to-all(f32[16,9,2,128]{3,2,1,0:T(2,128)S(1)} %bitcast.8), channel_id=1, replica_groups={{384,416,448,480,256,288,320,352,128,160,192,224,0,32,64,96},{385,417,4..., dimensions={0} | all-to-all | bytes 294912 | tf_op jit(solution)/shard_map/all_to_all | solution.py:254
  64.2 0.8 %shard_map.141 = (bf16[16,1024]{1,0:T(8,128)(2,1)}, bf16[16,1024]{1,0:T(8,128)(2,1)}, bf16[16,1024]{1,0:T(8,128)(2,1)}, f32[16,256]{1,0:T(8,128)}) custom-call(f32[288,128]{1,0:T(8,128)S(1)} %bitcast.10, bf16[16,1024]{1,0:T(8,128)(2,1)S(1)} %copy-done.4, bf16[16,1024]{1,0:T(8,128)(2,1)S(1)} %copy-done.5, bf16[16,1024]{1,0:T(8,128)(2,1)S(1)} %copy-done.6), custom_call_target="tpu_custom_call" | custom-call | tf_op jit(solution)/shard_map/pallas_call | solution.py:291
Async XLA Ops:
  0.6 0.8 %copy-start.4 = (bf16[16,1024]{1,0:T(8,128)(2,1)S(1)}, bf16[16,1024]{1,0:T(8,128)(2,1)}, u32[]{:S(2)}) copy-start(bf16[16,1024]{1,0:T(8,128)(2,1)} %k_ref.3) | copy-start | bytes 98308
  0.6 0.8 %copy-start.5 = (bf16[16,1024]{1,0:T(8,128)(2,1)S(1)}, bf16[16,1024]{1,0:T(8,128)(2,1)}, u32[]{:S(2)}) copy-start(bf16[16,1024]{1,0:T(8,128)(2,1)} %v_ref.3) | copy-start | bytes 98308
  0.7 0.8 %copy-start.6 = (bf16[16,1024]{1,0:T(8,128)(2,1)S(1)}, bf16[16,1024]{1,0:T(8,128)(2,1)}, u32[]{:S(2)}) copy-start(bf16[16,1024]{1,0:T(8,128)(2,1)} %g_ref.3) | copy-start | bytes 98308
  0.7 0.8 %copy-start.9 = (bf16[16,1024]{1,0:T(8,128)(2,1)S(1)}, bf16[16,1024]{1,0:T(8,128)(2,1)}, u32[]{:S(2)}) copy-start(bf16[16,1024]{1,0:T(8,128)(2,1)} %q_ref.1) | copy-start | bytes 98308
  0.7 0.8 %copy-start.10 = (f32[256,16]{0,1:T(8,128)S(1)}, f32[256,16]{0,1:T(8,128)}, u32[]{:S(2)}) copy-start(f32[256,16]{0,1:T(8,128)} %param.14) | copy-start | bytes 49156
  1.5 26.3 %copy-start = (bf16[768,256]{1,0:T(8,128)(2,1)S(1)}, bf16[768,256]{1,0:T(8,128)(2,1)}, u32[]{:S(2)}) copy-start(bf16[768,256]{1,0:T(8,128)(2,1)} %constant.21.clone.second_ref) | copy-start | bytes 1179652
  1.5 26.3 %copy-start.2 = (bf16[432,512]{1,0:T(8,128)(2,1)S(1)}, bf16[432,512]{1,0:T(8,128)(2,1)}, u32[]{:S(2)}) copy-start(bf16[432,512]{1,0:T(8,128)(2,1)} %constant.23.clone.lags_ref) | copy-start | bytes 1327108
  1.6 26.1 %copy-start.3 = (f32[2,72,128]{2,1,0:T(8,128)S(1)}, f32[2,72,128]{2,1,0:T(8,128)}, u32[]{:S(2)}) copy-start(f32[2,72,128]{2,1,0:T(8,128)} %constant.20.clone.twist_ref) | copy-start | bytes 221188
  1.6 26.1 %copy-start.7 = (bf16[144,192]{1,0:T(8,128)(2,1)S(1)}, bf16[144,192]{1,0:T(8,128)(2,1)}, u32[]{:S(2)}) copy-start(bf16[144,192]{1,0:T(8,128)(2,1)} %constant.18.clone.first_ref) | copy-start | bytes 165892
  27.8 15.4 %copy-start.1 = (bf16[144,1536]{1,0:T(8,128)(2,1)S(1)}, bf16[144,1536]{1,0:T(8,128)(2,1)}, u32[]{:S(2)}) copy-start(bf16[144,1536]{1,0:T(8,128)(2,1)} %constant.19.clone.taps_ref) | copy-start | bytes 1327108
  29.0 14.1 %copy-start.8 = (bf16[64,432]{1,0:T(8,128)(2,1)S(1)}, bf16[64,432]{1,0:T(8,128)(2,1)}, u32[]{:S(2)}) copy-start(bf16[64,432]{1,0:T(8,128)(2,1)} %constant.22.clone.last_ref) | copy-start | bytes 165892

commit v6 on v5

--- a/solution.py
+++ b/solution.py
@@ -16,7 +16,7 @@
 
 
 LEAD = 12
-LEAD_PLACE = 12
+LEAD_PLACE = 20
 
 
 def split_table(table):
@@ -35,14 +35,12 @@
     angle = turn * (k1[:, None] * t1[None, :] % 128)
     first = np.concatenate([live[:, None] * np.cos(angle), -live[:, None] * np.sin(angle)])
     high, low = split_table(first)
-    first3 = np.concatenate([high, high, low], axis=1)
+    first2 = np.concatenate([high, low])
 
     sources = np.arange(16) ^ LEAD
-    taps3 = []
-    for part in range(4):
-        high, low = split_table(np.tile(first[:, 4 * sources + part], (1, 8)))
-        taps3 += [high, high, low]
-    taps3 = np.concatenate(taps3, axis=1)
+    places = np.concatenate([4 * sources + part for part in range(4)])
+    high, low = split_table(first[:, places])
+    taps2 = np.concatenate([high, low])
 
     angle = 2 * np.pi / N * (k1[:, None] * t2[None, :] % N)
     twist = np.stack([live[:, None] * np.cos(angle), live[:, None] * np.sin(angle)]).astype(np.float32)
@@ -51,17 +49,21 @@
     cos, sin = np.cos(angle), np.sin(angle)
     second = np.block([[cos, -sin], [sin, cos]])
     high, low = split_table(second)
-    second3 = np.concatenate([high, low, high], axis=0)
+    second2 = np.concatenate([high, low])
+    mixed = (np.arange(128) % 8) * 16 + np.arange(128) // 8
+    both = np.concatenate([mixed, 128 + mixed])
+    lags_second = np.concatenate(split_table(second[:, both]))
+    taps_second = np.concatenate(split_table(second[both]))
+    mixed_twist = twist[:, :, mixed]
 
     weight = live * np.where((k1 == 0) | (k1 == 64), 1.0, 2.0) / N
     angle = turn * (t1[:, None] * k1[None, :] % 128)
     last = np.concatenate([weight * np.cos(angle), weight * np.sin(angle)], axis=1)
     high, low = split_table(last)
-    last3 = np.concatenate([high, high, low], axis=1)
-    lags = np.concatenate([np.tile(last[4 * sources + part].T, (1, 8)) for part in range(4)], axis=1)
-    high, low = split_table(lags)
-    lags3 = np.concatenate([high, low, high], axis=0)
-    return first3, taps3, twist, second3, last3, lags3
+    last2 = np.concatenate([high, low])
+    high, low = split_table(last[places])
+    lags2 = np.concatenate([high, low])
+    return first2, taps2, twist, second2, last2, lags2, mixed_twist, lags_second, taps_second
 
 
 def halves(x):
@@ -69,21 +71,6 @@
     return high, (x - high.astype(F32)).astype(BF16)
 
 
-def lanes3(x):
-    high, low = halves(x)
-    return jnp.concatenate([high, low, high], axis=1)
-
-
-def lanes3_table_last(x):
-    high, low = halves(x)
-    return jnp.concatenate([high, high, low], axis=1)
-
-
-def rows3(x):
-    high, low = halves(x)
-    return jnp.concatenate([high, low, high], axis=0)
-
-
 def mm(a, b):
     return jnp.dot(a, b, preferred_element_type=F32)
 
@@ -93,8 +80,18 @@
     return x_re * cos + x_im * sin, x_im * cos - x_re * sin
 
 
-def second_stage(stacked, second_ref):
-    return mm(lanes3_table_last(stacked), second_ref[...])
+def times_data(table_ref, data):
+    rows = table_ref.shape[0] // 2
+    high, low = halves(data)
+    both = mm(table_ref[...], high)
+    return both[:rows] + (both[rows:] + mm(table_ref[:rows, :], low))
+
+
+def second_stage(data, second_ref):
+    rows = data.shape[0]
+    high, low = halves(data)
+    both = mm(jnp.concatenate([high, low], axis=0), second_ref[:256, :])
+    return both[:rows] + (both[rows:] + mm(high, second_ref[256:, :]))
 
 
 def lane_group(width, rows):
@@ -130,14 +127,28 @@
     return (block * 2 + chan ^ LEAD) * MSG + array * 8
 
 
-def forward_kernel(in_ref, first_ref, twist_ref, second_ref, lags_ref, spec_ref, out_ref, taps_t, lags_t):
+def spread(values):
+    return jnp.concatenate([values] * 8, axis=0).T
+
+
+def gathered(values):
+    flipped = values.T
+    total = flipped[:16]
+    for a in range(1, 8):
+        total += flipped[a * 16 : a * 16 + 16]
+    return total
+
+
+def forward_kernel(
+    in_ref, first_ref, twist_ref, second_ref, lags_ref, mixed_ref, lags_second_ref, spec_ref, out_ref, taps_t
+):
     columns = []
     for array in range(2):
         for chan in range(2):
             starts = [message_start(block, chan, array) for block in range(8)]
             columns.append(jnp.concatenate([in_ref[start : start + 8, :] for start in starts], axis=0))
     signals = jnp.concatenate(columns, axis=1)
-    section = mm(first_ref[...], rows3(signals))
+    section = times_data(first_ref, signals)
     stacked = []
     for s in range(4):
         cols = slice(s * 128, s * 128 + 128)
@@ -153,18 +164,14 @@
         g = spec[(2 + chan) * ROWS : (2 + chan) * ROWS + ROWS]
         sum_re += g[:, :128] * x[:, :128] + g[:, 128:] * x[:, 128:]
         sum_im += g[:, :128] * x[:, 128:] - g[:, 128:] * x[:, :128]
-    back = second_stage(jnp.concatenate([sum_re, sum_im], axis=1), second_ref)
-    re, im = turned(back[:, :128], back[:, 128:], twist_ref)
-    flipped = jnp.concatenate([re, im], axis=0).T
-    lags = mm(lanes3_table_last(flipped), lags_ref[...]) * np.float32(1.0 / np.sqrt(32768.0))
-    for part in range(4):
-        lags_t[part * 128 : part * 128 + 128, :] = lags[:, part * 128 : part * 128 + 128]
-
+    back = second_stage(jnp.concatenate([sum_re, sum_im], axis=1), lags_second_ref)
+    re, im = turned(back[:, :128], back[:, 128:], mixed_ref)
+    lags = times_data(lags_ref, jnp.concatenate([re, im], axis=0)) * np.float32(1.0 / np.sqrt(32768.0))
     group = lane_group(16, 8)
     zero = jnp.zeros((8, 128), F32)
     for high in range(2):
         taps = in_ref[pl.ds(16 + high, 16, stride=MSG), :]
-        taps_t[...] = jnp.concatenate([taps] * 8, axis=0).T
+        taps_t[...] = spread(taps)
         for b in range(2):
             row = zero
             for a in range(8):
@@ -172,36 +179,38 @@
             for low in range(2):
                 put_places(out_ref, low * 2 + high, b, row)
     for part in range(4):
+        lags_t = spread(lags[part * 16 : part * 16 + 16])
         for b in range(2):
             row = zero
             for a in range(8):
-                row = jnp.where(group == a, lags_t[pl.ds(part * 128 + 2 * a + b, 8, stride=16), :], row)
+                start = (2 * a + b) * 8
+                row = jnp.where(group == a, lags_t[start : start + 8], row)
             put_places(out_ref, part, 2 + b, row)
 
 
-def backward_kernel(in_ref, spec_ref, taps_ref, twist_ref, second_ref, last_ref, out_ref, taps_t, lags_t):
+def backward_kernel(
+    in_ref, spec_ref, taps_ref, twist_ref, second_ref, last_ref, mixed_ref, taps_second_ref, out_ref, lags_t
+):
     group = lane_group(16, 16)
     for b in range(2):
-        for low in range(2):
-            row = get_places(in_ref, low, b)
-            for a in range(8):
-                taps_t[pl.ds(low * 256 + 2 * a + b, 16, stride=16), :] = jnp.where(group == a, row, 0.0)
         row = get_places(in_ref, 0, 2 + b) + get_places(in_ref, 1, 2 + b)
         for a in range(8):
             lags_t[pl.ds(2 * a + b, 16, stride=16), :] = jnp.where(group == a, row, 0.0)
     for high in range(2):
-        flipped = lags_t[high * 128 : high * 128 + 128, :].T
-        total = flipped[:16]
-        for a in range(1, 8):
-            total += flipped[a * 16 : a * 16 + 16]
-        out_ref[pl.ds(16 + high, 16, stride=MSG), :] = total
-
-    taps = jnp.concatenate([lanes3(taps_t[part * 128 : part * 128 + 128, :]) for part in range(4)], axis=1)
-    section = lax.dot_general(
-        taps_ref[...], taps, (((1,), (1,)), ((), ())), preferred_element_type=F32
-    )
-    re, im = turned(section[:ROWS], section[ROWS:], twist_ref)
-    filt = second_stage(jnp.concatenate([re, im], axis=1), second_ref)
+        out_ref[pl.ds(16 + high, 16, stride=MSG), :] = gathered(lags_t[high * 128 : high * 128 + 128, :])
+
+    parts = []
+    for low in range(2):
+        rows = [get_places(in_ref, low, b) for b in range(2)]
+        for high in range(2):
+            pieces = [
+                jnp.where(group[:8] == a, rows[b][high * 8 : high * 8 + 8], 0.0) for a in range(8) for b in range(2)
+            ]
+            parts.append(gathered(jnp.concatenate(pieces, axis=0)))
+    taps = jnp.concatenate(parts, axis=0)
+    section = times_data(taps_ref, taps)
+    re, im = turned(section[:ROWS], section[ROWS:], mixed_ref)
+    filt = second_stage(jnp.concatenate([re, im], axis=1), taps_second_ref)
     h_re, h_im = filt[:, :128], filt[:, 128:]
 
     products = []
@@ -217,7 +226,7 @@
         part = back[s * ROWS : s * ROWS + ROWS]
         re, im = turned(part[:, :128], part[:, 128:], twist_ref)
         columns.append(jnp.concatenate([re, im], axis=0))
-    landed = mm(last_ref[...], rows3(jnp.concatenate(columns, axis=1)))
+    landed = times_data(last_ref, jnp.concatenate(columns, axis=1))
     for s in range(4):
         array, chan = s // 2, s % 2
         for block in range(8):
@@ -256,7 +265,9 @@
 
 
 def on_device(q, k, v, filters, g):
-    first3, taps3, twist, second3, last3, lags3 = (jnp.asarray(t) for t in tables())
+    first2, taps2, twist, second2, last2, lags2, mixed_twist, lags_second, taps_second = (
+        jnp.asarray(t) for t in tables()
+    )
     place = jnp.broadcast_to(lax.axis_index("x").astype(F32), (2048, 128))
     packed = pl.pallas_call(
         pack_kernel,
@@ -270,21 +281,21 @@
     spec, sent = pl.pallas_call(
         forward_kernel,
         out_shape=(shape(4 * ROWS, 256), shape(128, 128)),
-        in_specs=[VMEM] * 5,
+        in_specs=[VMEM] * 7,
         out_specs=(VMEM, VMEM),
-        scratch_shapes=[pltpu.VMEM((128, 128), F32), pltpu.VMEM((512, 128), F32)],
+        scratch_shapes=[pltpu.VMEM((128, 128), F32)],
         compiler_params=PARAMS,
-    )(arrived, first3, twist, second3, lags3)
+    )(arrived, first2, twist, second2, lags2, mixed_twist, lags_second)
     swapped = exchange(sent, ("zgl", "zb", "y", "core"), 32, LEAD_PLACE)
 
     landed = pl.pallas_call(
         backward_kernel,
         out_shape=shape(16 * MSG, 128),
-        in_specs=[VMEM] * 6,
+        in_specs=[VMEM] * 8,
         out_specs=VMEM,
-        scratch_shapes=[pltpu.VMEM((512, 128), F32), pltpu.VMEM((256, 128), F32)],
+        scratch_shapes=[pltpu.VMEM((256, 128), F32)],
         compiler_params=PARAMS,
-    )(swapped, spec, taps3, twist, second3, last3)
+    )(swapped, spec, taps2, twist, second2, last2, mixed_twist, taps_second)
     home = exchange(landed, ("zh", "x", "zgh"), 16, LEAD)
 
     out = shape(*q.shape, dtype=BF16)

time: 65.3 us -> 64.3 us (0.985)
  blocking collectives: 60.1 us -> 59.4 us
    all_to_all x3, blocking collectives: 60.1 us -> 59.4 us  [exchange(): lax.all_to_all(messages, axes, split_axis=0, concat_axis=0, axis_index_gr...]
where the time goes in v6:
time: 64.3 us; the launch traced here: 64 us
  blocking collectives  59.4 us (92%)
  Pallas kernels  3.01 us (5%)
  local copies, waits for them, and re-layouts  0.82 us (1%)
  between operations  0.79 us (1%)
    all_to_all x3, blocking collectives, exchange(): lax.all_to_all(messages, axes, split_axis=0, concat_axis=0, axis_index_gr...  59.4 us

profile of v6, /device:TPU:1, one launch (start us, length us, event | category | flops | bytes accessed | tf_op | source)
XLA Modules:
  0.0 64.0 jit_solution(8789709412205046400)
XLA Ops:
  0.6 0.0 copy-start.5
  0.6 0.0 copy-start.6
  0.7 0.0 copy-start.7
  0.7 0.0 copy-start.12
  0.7 0.0 copy-start.13
  0.7 0.1 broadcast_in_dim.3.place_ref
  0.8 0.6 copy-done.5
  1.4 0.0 copy-done.6
  1.4 0.0 copy-done.7
  1.4 0.0 copy-done.12
  1.4 0.0 copy-done.13
  1.5 0.0 copy-start.1
  1.5 0.0 copy-start.2
  1.5 0.0 copy-start.4
  1.5 0.0 copy-start.9
  1.5 0.0 copy-start.11
  1.5 0.2 shard_map.165
  1.7 0.0 copy-start
  1.7 26.1 %all_to_all.15 = f32[16,9,2,128]{3,2,1,0:T(2,128)S(1)} all-to-all(f32[16,9,2,128]{3,2,1,0:T(2,128)S(1)} %bitcast.10), channel_id=1, replica_groups={{384,416,448,480,256,288,320,352,128,160,192,224,0,32,64,96},{385,417,4..., dimensions={0} | all-to-all | bytes 294912 | tf_op jit(solution)/shard_map/all_to_all | solution.py:263
  27.8 0.0 copy-done.1
  27.8 0.0 copy-done.2
  27.8 0.0 copy-done.4
  27.8 0.0 copy-done.9
  27.8 0.0 copy-done.11
  27.8 0.0 copy-done
  27.8 0.0 copy-start.3
  27.8 0.0 copy-start.10
  27.8 1.1 %shard_map.166 = (f32[288,256]{1,0:T(8,128)S(1)}, f32[128,128]{1,0:T(8,128)S(1)}) custom-call(f32[288,128]{1,0:T(8,128)S(1)} %bitcast.11, bf16[288,64]{1,0:T(8,128)(2,1)S(1)} %copy-done.9, f32[2,72,128]{2,1,0:T(8,128)S(1)} %copy-done.2, bf16[512,256]{1,0:T(8,128)(2,1)S(1)} %copy-done, bf16[128,144]{1,0:T(8,128)(2,1)S(1)} %copy-done.11, ...), custom_call_target="tpu_custom_call" | custom-call | tf_op jit(solution)/shard_map/pallas_call | solution.py:281
  28.9 0.0 copy-start.8
  28.9 13.2 %all_to_all.16 = f32[32,2,2,128]{3,2,1,0:T(2,128)S(1)} all-to-all(f32[32,2,2,128]{3,2,1,0:T(2,128)S(1)} %bitcast.13), channel_id=1, replica_groups={{20,21,22,23,16,17,18,19,28,29,30,31,24,25,26,27,4,5,6,7,0,1,2,3,12,13,..., dimensions={0} | all-to-all | bytes 131072 | tf_op jit(solution)/shard_map/all_to_all | solution.py:263
  42.1 0.0 copy-done.3
  42.1 0.0 copy-done.10
  42.1 0.0 copy-done.8
  42.1 1.0 %shard_map.167 = f32[288,128]{1,0:T(8,128)S(1)} custom-call(f32[128,128]{1,0:T(8,128)S(1)} %bitcast.12, f32[288,256]{1,0:T(8,128)S(1)} %get-tuple-element.11.spec_ref, bf16[288,64]{1,0:T(8,128)(2,1)S(1)} %copy-done.8, f32[2,72,128]{2,1,0:T(8,128)S(1)} %copy-done.2, bf16[512,256]{1,0:T(8,128)(2,1)S(1)} %copy-done, bf16[128,144]{1,0:T(8,128)(2,1)S(1)} %copy-done.10, ...), custom_call_target="tpu_custom_call" | custom-call | tf_op jit(solution)/shard_map/pallas_call | solution.py:291
  43.1 20.1 %all_to_all.17 = f32[16,9,2,128]{3,2,1,0:T(2,128)S(1)} all-to-all(f32[16,9,2,128]{3,2,1,0:T(2,128)S(1)} %bitcast.8), channel_id=1, replica_groups={{384,416,448,480,256,288,320,352,128,160,192,224,0,32,64,96},{385,417,4..., dimensions={0} | all-to-all | bytes 294912 | tf_op jit(solution)/shard_map/all_to_all | solution.py:263
  63.2 0.8 %shard_map.168 = (bf16[16,1024]{1,0:T(8,128)(2,1)}, bf16[16,1024]{1,0:T(8,128)(2,1)}, bf16[16,1024]{1,0:T(8,128)(2,1)}, f32[16,256]{1,0:T(8,128)}) custom-call(f32[288,128]{1,0:T(8,128)S(1)} %bitcast.9, bf16[16,1024]{1,0:T(8,128)(2,1)S(1)} %copy-done.5, bf16[16,1024]{1,0:T(8,128)(2,1)S(1)} %copy-done.6, bf16[16,1024]{1,0:T(8,128)(2,1)S(1)} %copy-done.7), custom_call_target="tpu_custom_call" | custom-call | tf_op jit(solution)/shard_map/pallas_call | solution.py:302
Async XLA Ops:
  0.6 0.8 %copy-start.5 = (bf16[16,1024]{1,0:T(8,128)(2,1)S(1)}, bf16[16,1024]{1,0:T(8,128)(2,1)}, u32[]{:S(2)}) copy-start(bf16[16,1024]{1,0:T(8,128)(2,1)} %k_ref.3) | copy-start | bytes 98308
  0.6 0.8 %copy-start.6 = (bf16[16,1024]{1,0:T(8,128)(2,1)S(1)}, bf16[16,1024]{1,0:T(8,128)(2,1)}, u32[]{:S(2)}) copy-start(bf16[16,1024]{1,0:T(8,128)(2,1)} %v_ref.3) | copy-start | bytes 98308
  0.7 0.8 %copy-start.7 = (bf16[16,1024]{1,0:T(8,128)(2,1)S(1)}, bf16[16,1024]{1,0:T(8,128)(2,1)}, u32[]{:S(2)}) copy-start(bf16[16,1024]{1,0:T(8,128)(2,1)} %g_ref.3) | copy-start | bytes 98308
  0.7 0.8 %copy-start.12 = (bf16[16,1024]{1,0:T(8,128)(2,1)S(1)}, bf16[16,1024]{1,0:T(8,128)(2,1)}, u32[]{:S(2)}) copy-start(bf16[16,1024]{1,0:T(8,128)(2,1)} %q_ref.1) | copy-start | bytes 98308
  0.7 0.8 %copy-start.13 = (f32[256,16]{0,1:T(8,128)S(1)}, f32[256,16]{0,1:T(8,128)}, u32[]{:S(2)}) copy-start(f32[256,16]{0,1:T(8,128)} %param.17) | copy-start | bytes 49156
  1.5 26.3 %copy-start.1 = (f32[2,72,128]{2,1,0:T(8,128)S(1)}, f32[2,72,128]{2,1,0:T(8,128)}, u32[]{:S(2)}) copy-start(f32[2,72,128]{2,1,0:T(8,128)} %constant.30.clone.mixed_ref) | copy-start | bytes 221188
  1.5 26.3 %copy-start.2 = (f32[2,72,128]{2,1,0:T(8,128)S(1)}, f32[2,72,128]{2,1,0:T(8,128)}, u32[]{:S(2)}) copy-start(f32[2,72,128]{2,1,0:T(8,128)} %constant.26.clone.twist_ref) | copy-start | bytes 221188
  1.5 26.3 %copy-start.4 = (bf16[512,256]{1,0:T(8,128)(2,1)S(1)}, bf16[512,256]{1,0:T(8,128)(2,1)}, u32[]{:S(2)}) copy-start(bf16[512,256]{1,0:T(8,128)(2,1)} %constant.31.clone.lags_second_ref) | copy-start | bytes 786436
  1.5 26.3 %copy-start.9 = (bf16[288,64]{1,0:T(8,128)(2,1)S(1)}, bf16[288,64]{1,0:T(8,128)(2,1)}, u32[]{:S(2)}) copy-start(bf16[288,64]{1,0:T(8,128)(2,1)} %constant.24.clone.first_ref) | copy-start | bytes 110596
  1.5 26.3 %copy-start.11 = (bf16[128,144]{1,0:T(8,128)(2,1)S(1)}, bf16[128,144]{1,0:T(8,128)(2,1)}, u32[]{:S(2)}) copy-start(bf16[128,144]{1,0:T(8,128)(2,1)} %constant.29.clone.lags_ref) | copy-start | bytes 110596
  1.7 26.1 %copy-start = (bf16[512,256]{1,0:T(8,128)(2,1)S(1)}, bf16[512,256]{1,0:T(8,128)(2,1)}, u32[]{:S(2)}) copy-start(bf16[512,256]{1,0:T(8,128)(2,1)} %constant.27.clone.second_ref) | copy-start | bytes 786436
  27.8 14.3 %copy-start.3 = (bf16[512,256]{1,0:T(8,128)(2,1)S(1)}, bf16[512,256]{1,0:T(8,128)(2,1)}, u32[]{:S(2)}) copy-start(bf16[512,256]{1,0:T(8,128)(2,1)} %constant.32.clone.taps_second_ref) | copy-start | bytes 786436
  27.8 14.3 %copy-start.10 = (bf16[128,144]{1,0:T(8,128)(2,1)S(1)}, bf16[128,144]{1,0:T(8,128)(2,1)}, u32[]{:S(2)}) copy-start(bf16[128,144]{1,0:T(8,128)(2,1)} %constant.28.clone.last_ref) | copy-start | bytes 110596
  28.9 13.2 %copy-start.8 = (bf16[288,64]{1,0:T(8,128)(2,1)S(1)}, bf16[288,64]{1,0:T(8,128)(2,1)}, u32[]{:S(2)}) copy-start(bf16[288,64]{1,0:T(8,128)(2,1)} %constant.25.clone.taps_ref) | copy-start | bytes 110596

commit v7 on v6

--- a/solution.py
+++ b/solution.py
@@ -15,7 +15,7 @@
 MSG = 18
 
 
-LEAD = 12
+ORDER = [12, 11, 13, 8, 14, 10, 6, 1, 4, 7, 15, 5, 9, 2, 3, 0]
 LEAD_PLACE = 20
 
 
@@ -37,7 +37,7 @@
     high, low = split_table(first)
     first2 = np.concatenate([high, low])
 
-    sources = np.arange(16) ^ LEAD
+    sources = np.array(ORDER)
     places = np.concatenate([4 * sources + part for part in range(4)])
     high, low = split_table(first[:, places])
     taps2 = np.concatenate([high, low])
@@ -85,6 +85,13 @@
     high, low = halves(data)
     both = mm(table_ref[...], high)
     return both[:rows] + (both[rows:] + mm(table_ref[:rows, :], low))
+
+
+def times_data_once(table_ref, data):
+    rows = table_ref.shape[0] // 2
+    high, low = halves(data)
+    table = jnp.concatenate([table_ref[:rows, :], table_ref[:rows, :], table_ref[rows:, :]], axis=1)
+    return mm(table, jnp.concatenate([high, low, high], axis=0))
 
 
 def second_stage(data, second_ref):
@@ -124,7 +131,7 @@
 
 
 def message_start(block, chan, array):
-    return (block * 2 + chan ^ LEAD) * MSG + array * 8
+    return ORDER.index(block * 2 + chan) * MSG + array * 8
 
 
 def spread(values):
@@ -148,7 +155,7 @@
             starts = [message_start(block, chan, array) for block in range(8)]
             columns.append(jnp.concatenate([in_ref[start : start + 8, :] for start in starts], axis=0))
     signals = jnp.concatenate(columns, axis=1)
-    section = times_data(first_ref, signals)
+    section = times_data_once(first_ref, signals)
     stacked = []
     for s in range(4):
         cols = slice(s * 128, s * 128 + 128)
@@ -257,9 +264,8 @@
     return jax.ShapeDtypeStruct(dims, dtype)
 
 
-def exchange(rows, axes, count, lead):
-    messages = rows.reshape(count, rows.shape[0] // count // 2, 2, 128)
-    slots = [slot ^ lead for slot in range(count)]
+def exchange(rows, axes, slots):
+    messages = rows.reshape(len(slots), rows.shape[0] // len(slots) // 2, 2, 128)
     arrived = lax.all_to_all(messages, axes, split_axis=0, concat_axis=0, axis_index_groups=[slots], tiled=True)
     return arrived.reshape(rows.shape)
 
@@ -276,7 +282,7 @@
         out_specs=VMEM,
         compiler_params=PARAMS,
     )(place, q, k, v, g, filters.T)
-    arrived = exchange(packed, ("zh", "x", "zgh"), 16, LEAD)
+    arrived = exchange(packed, ("zh", "x", "zgh"), ORDER)
 
     spec, sent = pl.pallas_call(
         forward_kernel,
@@ -286,7 +292,7 @@
         scratch_shapes=[pltpu.VMEM((128, 128), F32)],
         compiler_params=PARAMS,
     )(arrived, first2, twist, second2, lags2, mixed_twist, lags_second)
-    swapped = exchange(sent, ("zgl", "zb", "y", "core"), 32, LEAD_PLACE)
+    swapped = exchange(sent, ("zgl", "zb", "y", "core"), [slot ^ LEAD_PLACE for slot in range(32)])
 
     landed = pl.pallas_call(
         backward_kernel,
@@ -296,7 +302,7 @@
         scratch_shapes=[pltpu.VMEM((256, 128), F32)],
         compiler_params=PARAMS,
     )(swapped, spec, taps2, twist, second2, last2, mixed_twist, taps_second)
-    home = exchange(landed, ("zh", "x", "zgh"), 16, LEAD)
+    home = exchange(landed, ("zh", "x", "zgh"), ORDER)
 
     out = shape(*q.shape, dtype=BF16)
     q_grad, k_grad, v_grad, f_grad = pl.pallas_call(

time: 64.3 us -> 63.6 us (0.989)
  blocking collectives: 59.4 us -> 58.6 us
    all_to_all x3, blocking collectives: 59.4 us -> 58.6 us  [exchange(): lax.all_to_all(messages, axes, split_axis=0, concat_axis=0, axis_index_gr...]
where the time goes in v7:
time: 63.6 us; the launch traced here: 63.2 us
  blocking collectives  58.6 us (92%)
  Pallas kernels  2.93 us (5%)
  local copies, waits for them, and re-layouts  0.82 us (1%)
  between operations  0.79 us (1%)
    all_to_all x3, blocking collectives, exchange(): lax.all_to_all(messages, axes, split_axis=0, concat_axis=0, axis_index_gr...  58.6 us

profile of v7, /device:TPU:1, one launch (start us, length us, event | category | flops | bytes accessed | tf_op | source)
XLA Modules:
  0.0 63.2 jit_solution(682777882440958167)
XLA Ops:
  0.6 0.0 copy-start.5
  0.6 0.0 copy-start.6
  0.7 0.0 copy-start.7
  0.7 0.0 copy-start.12
  0.7 0.0 copy-start.13
  0.7 0.1 broadcast_in_dim.3.place_ref
  0.8 0.6 copy-done.5
  1.4 0.0 copy-done.6
  1.4 0.0 copy-done.7
  1.4 0.0 copy-done.12
  1.4 0.0 copy-done.13
  1.5 0.0 copy-start.1
  1.5 0.0 copy-start.2
  1.5 0.0 copy-start.4
  1.5 0.0 copy-start.9
  1.5 0.0 copy-start.11
  1.5 0.2 shard_map.165
  1.7 0.0 copy-start
  1.7 25.8 %all_to_all.15 = f32[16,9,2,128]{3,2,1,0:T(2,128)S(1)} all-to-all(f32[16,9,2,128]{3,2,1,0:T(2,128)S(1)} %bitcast.10), channel_id=1, replica_groups={{384,352,416,256,448,320,192,32,128,224,480,160,288,64,96,0},{385,353,4..., dimensions={0} | all-to-all | bytes 294912 | tf_op jit(solution)/shard_map/all_to_all | solution.py:269
  27.5 0.0 copy-done.1
  27.5 0.0 copy-done.2
  27.5 0.0 copy-done.4
  27.5 0.0 copy-done.9
  27.5 0.0 copy-done.11
  27.5 0.0 copy-done
  27.5 0.0 copy-start.3
  27.6 0.0 copy-start.10
  27.6 1.0 %shard_map.166 = (f32[288,256]{1,0:T(8,128)S(1)}, f32[128,128]{1,0:T(8,128)S(1)}) custom-call(f32[288,128]{1,0:T(8,128)S(1)} %bitcast.11, bf16[288,64]{1,0:T(8,128)(2,1)S(1)} %copy-done.9, f32[2,72,128]{2,1,0:T(8,128)S(1)} %copy-done.2, bf16[512,256]{1,0:T(8,128)(2,1)S(1)} %copy-done, bf16[128,144]{1,0:T(8,128)(2,1)S(1)} %copy-done.11, ...), custom_call_target="tpu_custom_call" | custom-call | tf_op jit(solution)/shard_map/pallas_call | solution.py:287
  28.6 0.0 copy-start.8
  28.6 13.5 %all_to_all.16 = f32[32,2,2,128]{3,2,1,0:T(2,128)S(1)} all-to-all(f32[32,2,2,128]{3,2,1,0:T(2,128)S(1)} %bitcast.13), channel_id=1, replica_groups={{20,21,22,23,16,17,18,19,28,29,30,31,24,25,26,27,4,5,6,7,0,1,2,3,12,13,..., dimensions={0} | all-to-all | bytes 131072 | tf_op jit(solution)/shard_map/all_to_all | solution.py:269
  42.1 0.0 copy-done.3
  42.1 0.0 copy-done.10
  42.1 0.0 copy-done.8
  42.1 1.0 %shard_map.167 = f32[288,128]{1,0:T(8,128)S(1)} custom-call(f32[128,128]{1,0:T(8,128)S(1)} %bitcast.12, f32[288,256]{1,0:T(8,128)S(1)} %get-tuple-element.11.spec_ref, bf16[288,64]{1,0:T(8,128)(2,1)S(1)} %copy-done.8, f32[2,72,128]{2,1,0:T(8,128)S(1)} %copy-done.2, bf16[512,256]{1,0:T(8,128)(2,1)S(1)} %copy-done, bf16[128,144]{1,0:T(8,128)(2,1)S(1)} %copy-done.10, ...), custom_call_target="tpu_custom_call" | custom-call | tf_op jit(solution)/shard_map/pallas_call | solution.py:297
  43.1 19.3 %all_to_all.17 = f32[16,9,2,128]{3,2,1,0:T(2,128)S(1)} all-to-all(f32[16,9,2,128]{3,2,1,0:T(2,128)S(1)} %bitcast.8), channel_id=1, replica_groups={{384,352,416,256,448,320,192,32,128,224,480,160,288,64,96,0},{385,353,4..., dimensions={0} | all-to-all | bytes 294912 | tf_op jit(solution)/shard_map/all_to_all | solution.py:269
  62.4 0.8 %shard_map.168 = (bf16[16,1024]{1,0:T(8,128)(2,1)}, bf16[16,1024]{1,0:T(8,128)(2,1)}, bf16[16,1024]{1,0:T(8,128)(2,1)}, f32[16,256]{1,0:T(8,128)}) custom-call(f32[288,128]{1,0:T(8,128)S(1)} %bitcast.9, bf16[16,1024]{1,0:T(8,128)(2,1)S(1)} %copy-done.5, bf16[16,1024]{1,0:T(8,128)(2,1)S(1)} %copy-done.6, bf16[16,1024]{1,0:T(8,128)(2,1)S(1)} %copy-done.7), custom_call_target="tpu_custom_call" | custom-call | tf_op jit(solution)/shard_map/pallas_call | solution.py:308
Async XLA Ops:
  0.6 0.8 %copy-start.5 = (bf16[16,1024]{1,0:T(8,128)(2,1)S(1)}, bf16[16,1024]{1,0:T(8,128)(2,1)}, u32[]{:S(2)}) copy-start(bf16[16,1024]{1,0:T(8,128)(2,1)} %k_ref.3) | copy-start | bytes 98308
  0.6 0.8 %copy-start.6 = (bf16[16,1024]{1,0:T(8,128)(2,1)S(1)}, bf16[16,1024]{1,0:T(8,128)(2,1)}, u32[]{:S(2)}) copy-start(bf16[16,1024]{1,0:T(8,128)(2,1)} %v_ref.3) | copy-start | bytes 98308
  0.7 0.8 %copy-start.7 = (bf16[16,1024]{1,0:T(8,128)(2,1)S(1)}, bf16[16,1024]{1,0:T(8,128)(2,1)}, u32[]{:S(2)}) copy-start(bf16[16,1024]{1,0:T(8,128)(2,1)} %g_ref.3) | copy-start | bytes 98308
  0.7 0.8 %copy-start.12 = (bf16[16,1024]{1,0:T(8,128)(2,1)S(1)}, bf16[16,1024]{1,0:T(8,128)(2,1)}, u32[]{:S(2)}) copy-start(bf16[16,1024]{1,0:T(8,128)(2,1)} %q_ref.1) | copy-start | bytes 98308
  0.7 0.8 %copy-start.13 = (f32[256,16]{0,1:T(8,128)S(1)}, f32[256,16]{0,1:T(8,128)}, u32[]{:S(2)}) copy-start(f32[256,16]{0,1:T(8,128)} %param.17) | copy-start | bytes 49156
  1.5 26.1 %copy-start.1 = (f32[2,72,128]{2,1,0:T(8,128)S(1)}, f32[2,72,128]{2,1,0:T(8,128)}, u32[]{:S(2)}) copy-start(f32[2,72,128]{2,1,0:T(8,128)} %constant.30.clone.mixed_ref) | copy-start | bytes 221188
  1.5 26.1 %copy-start.2 = (f32[2,72,128]{2,1,0:T(8,128)S(1)}, f32[2,72,128]{2,1,0:T(8,128)}, u32[]{:S(2)}) copy-start(f32[2,72,128]{2,1,0:T(8,128)} %constant.26.clone.twist_ref) | copy-start | bytes 221188
  1.5 26.1 %copy-start.4 = (bf16[512,256]{1,0:T(8,128)(2,1)S(1)}, bf16[512,256]{1,0:T(8,128)(2,1)}, u32[]{:S(2)}) copy-start(bf16[512,256]{1,0:T(8,128)(2,1)} %constant.31.clone.lags_second_ref) | copy-start | bytes 786436
  1.5 26.1 %copy-start.9 = (bf16[288,64]{1,0:T(8,128)(2,1)S(1)}, bf16[288,64]{1,0:T(8,128)(2,1)}, u32[]{:S(2)}) copy-start(bf16[288,64]{1,0:T(8,128)(2,1)} %constant.24.clone.first_ref) | copy-start | bytes 110596
  1.5 26.1 %copy-start.11 = (bf16[128,144]{1,0:T(8,128)(2,1)S(1)}, bf16[128,144]{1,0:T(8,128)(2,1)}, u32[]{:S(2)}) copy-start(bf16[128,144]{1,0:T(8,128)(2,1)} %constant.29.clone.lags_ref) | copy-start | bytes 110596
  1.7 25.9 %copy-start = (bf16[512,256]{1,0:T(8,128)(2,1)S(1)}, bf16[512,256]{1,0:T(8,128)(2,1)}, u32[]{:S(2)}) copy-start(bf16[512,256]{1,0:T(8,128)(2,1)} %constant.27.clone.second_ref) | copy-start | bytes 786436
  27.5 14.6 %copy-start.3 = (bf16[512,256]{1,0:T(8,128)(2,1)S(1)}, bf16[512,256]{1,0:T(8,128)(2,1)}, u32[]{:S(2)}) copy-start(bf16[512,256]{1,0:T(8,128)(2,1)} %constant.32.clone.taps_second_ref) | copy-start | bytes 786436
  27.6 14.6 %copy-start.10 = (bf16[128,144]{1,0:T(8,128)(2,1)S(1)}, bf16[128,144]{1,0:T(8,128)(2,1)}, u32[]{:S(2)}) copy-start(bf16[128,144]{1,0:T(8,128)(2,1)} %constant.28.clone.last_ref) | copy-start | bytes 110596
  28.6 13.6 %copy-start.8 = (bf16[288,64]{1,0:T(8,128)(2,1)S(1)}, bf16[288,64]{1,0:T(8,128)(2,1)}, u32[]{:S(2)}) copy-start(bf16[288,64]{1,0:T(8,128)(2,1)} %constant.25.clone.taps_ref) | copy-start | bytes 110596

commit v8 on v7

--- a/solution.py
+++ b/solution.py
@@ -15,7 +15,7 @@
 MSG = 18
 
 
-ORDER = [12, 11, 13, 8, 14, 10, 6, 1, 4, 7, 15, 5, 9, 2, 3, 0]
+ORDER = [12, 11, 13, 8, 14, 10, 15, 1, 4, 7, 6, 5, 9, 2, 3, 0]
 LEAD_PLACE = 20
 
 

time: 63.6 us -> 63.9 us (level)
  no operation moved by 1% of the time
where the time goes in v8:
time: 63.9 us; the launch traced here: 63.6 us
  blocking collectives  59 us (92%)
  Pallas kernels  2.93 us (5%)
  local copies, waits for them, and re-layouts  0.82 us (1%)
  between operations  0.79 us (1%)
    all_to_all x3, blocking collectives, exchange(): lax.all_to_all(messages, axes, split_axis=0, concat_axis=0, axis_index_gr...  59 us

profile of v8, /device:TPU:1, one launch (start us, length us, event | category | flops | bytes accessed | tf_op | source)
XLA Modules:
  0.0 63.6 jit_solution(17860278119855218254)
XLA Ops:
  0.6 0.0 copy-start.5
  0.6 0.0 copy-start.6
  0.7 0.0 copy-start.7
  0.7 0.0 copy-start.12
  0.7 0.0 copy-start.13
  0.7 0.1 broadcast_in_dim.3.place_ref
  0.8 0.6 copy-done.5
  1.4 0.0 copy-done.6
  1.4 0.0 copy-done.7
  1.4 0.0 copy-done.12
  1.4 0.0 copy-done.13
  1.5 0.0 copy-start.1
  1.5 0.0 copy-start.2
  1.5 0.0 copy-start.4
  1.5 0.0 copy-start.9
  1.5 0.0 copy-start.11
  1.5 0.2 shard_map.165
  1.7 0.0 copy-start
  1.7 26.1 %all_to_all.15 = f32[16,9,2,128]{3,2,1,0:T(2,128)S(1)} all-to-all(f32[16,9,2,128]{3,2,1,0:T(2,128)S(1)} %bitcast.10), channel_id=1, replica_groups={{384,352,416,256,448,320,480,32,128,224,192,160,288,64,96,0},{385,353,4..., dimensions={0} | all-to-all | bytes 294912 | tf_op jit(solution)/shard_map/all_to_all | solution.py:269
  27.8 0.0 copy-done.1
  27.8 0.0 copy-done.2
  27.8 0.0 copy-done.4
  27.8 0.0 copy-done.9
  27.8 0.0 copy-done.11
  27.8 0.0 copy-done
  27.8 0.0 copy-start.3
  27.8 0.0 copy-start.10
  27.8 1.0 %shard_map.166 = (f32[288,256]{1,0:T(8,128)S(1)}, f32[128,128]{1,0:T(8,128)S(1)}) custom-call(f32[288,128]{1,0:T(8,128)S(1)} %bitcast.11, bf16[288,64]{1,0:T(8,128)(2,1)S(1)} %copy-done.9, f32[2,72,128]{2,1,0:T(8,128)S(1)} %copy-done.2, bf16[512,256]{1,0:T(8,128)(2,1)S(1)} %copy-done, bf16[128,144]{1,0:T(8,128)(2,1)S(1)} %copy-done.11, ...), custom_call_target="tpu_custom_call" | custom-call | tf_op jit(solution)/shard_map/pallas_call | solution.py:287
  28.8 0.0 copy-start.8
  28.9 13.3 %all_to_all.16 = f32[32,2,2,128]{3,2,1,0:T(2,128)S(1)} all-to-all(f32[32,2,2,128]{3,2,1,0:T(2,128)S(1)} %bitcast.13), channel_id=1, replica_groups={{20,21,22,23,16,17,18,19,28,29,30,31,24,25,26,27,4,5,6,7,0,1,2,3,12,13,..., dimensions={0} | all-to-all | bytes 131072 | tf_op jit(solution)/shard_map/all_to_all | solution.py:269
  42.1 0.0 copy-done.3
  42.1 0.0 copy-done.10
  42.1 0.0 copy-done.8
  42.1 1.0 %shard_map.167 = f32[288,128]{1,0:T(8,128)S(1)} custom-call(f32[128,128]{1,0:T(8,128)S(1)} %bitcast.12, f32[288,256]{1,0:T(8,128)S(1)} %get-tuple-element.11.spec_ref, bf16[288,64]{1,0:T(8,128)(2,1)S(1)} %copy-done.8, f32[2,72,128]{2,1,0:T(8,128)S(1)} %copy-done.2, bf16[512,256]{1,0:T(8,128)(2,1)S(1)} %copy-done, bf16[128,144]{1,0:T(8,128)(2,1)S(1)} %copy-done.10, ...), custom_call_target="tpu_custom_call" | custom-call | tf_op jit(solution)/shard_map/pallas_call | solution.py:297
  43.1 19.6 %all_to_all.17 = f32[16,9,2,128]{3,2,1,0:T(2,128)S(1)} all-to-all(f32[16,9,2,128]{3,2,1,0:T(2,128)S(1)} %bitcast.8), channel_id=1, replica_groups={{384,352,416,256,448,320,480,32,128,224,192,160,288,64,96,0},{385,353,4..., dimensions={0} | all-to-all | bytes 294912 | tf_op jit(solution)/shard_map/all_to_all | solution.py:269
  62.8 0.8 %shard_map.168 = (bf16[16,1024]{1,0:T(8,128)(2,1)}, bf16[16,1024]{1,0:T(8,128)(2,1)}, bf16[16,1024]{1,0:T(8,128)(2,1)}, f32[16,256]{1,0:T(8,128)}) custom-call(f32[288,128]{1,0:T(8,128)S(1)} %bitcast.9, bf16[16,1024]{1,0:T(8,128)(2,1)S(1)} %copy-done.5, bf16[16,1024]{1,0:T(8,128)(2,1)S(1)} %copy-done.6, bf16[16,1024]{1,0:T(8,128)(2,1)S(1)} %copy-done.7), custom_call_target="tpu_custom_call" | custom-call | tf_op jit(solution)/shard_map/pallas_call | solution.py:308
Async XLA Ops:
  0.6 0.8 %copy-start.5 = (bf16[16,1024]{1,0:T(8,128)(2,1)S(1)}, bf16[16,1024]{1,0:T(8,128)(2,1)}, u32[]{:S(2)}) copy-start(bf16[16,1024]{1,0:T(8,128)(2,1)} %k_ref.3) | copy-start | bytes 98308
  0.6 0.8 %copy-start.6 = (bf16[16,1024]{1,0:T(8,128)(2,1)S(1)}, bf16[16,1024]{1,0:T(8,128)(2,1)}, u32[]{:S(2)}) copy-start(bf16[16,1024]{1,0:T(8,128)(2,1)} %v_ref.3) | copy-start | bytes 98308
  0.7 0.8 %copy-start.7 = (bf16[16,1024]{1,0:T(8,128)(2,1)S(1)}, bf16[16,1024]{1,0:T(8,128)(2,1)}, u32[]{:S(2)}) copy-start(bf16[16,1024]{1,0:T(8,128)(2,1)} %g_ref.3) | copy-start | bytes 98308
  0.7 0.8 %copy-start.12 = (bf16[16,1024]{1,0:T(8,128)(2,1)S(1)}, bf16[16,1024]{1,0:T(8,128)(2,1)}, u32[]{:S(2)}) copy-start(bf16[16,1024]{1,0:T(8,128)(2,1)} %q_ref.1) | copy-start | bytes 98308
  0.7 0.8 %copy-start.13 = (f32[256,16]{0,1:T(8,128)S(1)}, f32[256,16]{0,1:T(8,128)}, u32[]{:S(2)}) copy-start(f32[256,16]{0,1:T(8,128)} %param.17) | copy-start | bytes 49156
  1.5 26.3 %copy-start.1 = (f32[2,72,128]{2,1,0:T(8,128)S(1)}, f32[2,72,128]{2,1,0:T(8,128)}, u32[]{:S(2)}) copy-start(f32[2,72,128]{2,1,0:T(8,128)} %constant.30.clone.mixed_ref) | copy-start | bytes 221188
  1.5 26.3 %copy-start.2 = (f32[2,72,128]{2,1,0:T(8,128)S(1)}, f32[2,72,128]{2,1,0:T(8,128)}, u32[]{:S(2)}) copy-start(f32[2,72,128]{2,1,0:T(8,128)} %constant.26.clone.twist_ref) | copy-start | bytes 221188
  1.5 26.3 %copy-start.4 = (bf16[512,256]{1,0:T(8,128)(2,1)S(1)}, bf16[512,256]{1,0:T(8,128)(2,1)}, u32[]{:S(2)}) copy-start(bf16[512,256]{1,0:T(8,128)(2,1)} %constant.31.clone.lags_second_ref) | copy-start | bytes 786436
  1.5 26.3 %copy-start.9 = (bf16[288,64]{1,0:T(8,128)(2,1)S(1)}, bf16[288,64]{1,0:T(8,128)(2,1)}, u32[]{:S(2)}) copy-start(bf16[288,64]{1,0:T(8,128)(2,1)} %constant.24.clone.first_ref) | copy-start | bytes 110596
  1.5 26.3 %copy-start.11 = (bf16[128,144]{1,0:T(8,128)(2,1)S(1)}, bf16[128,144]{1,0:T(8,128)(2,1)}, u32[]{:S(2)}) copy-start(bf16[128,144]{1,0:T(8,128)(2,1)} %constant.29.clone.lags_ref) | copy-start | bytes 110596
  1.7 26.1 %copy-start = (bf16[512,256]{1,0:T(8,128)(2,1)S(1)}, bf16[512,256]{1,0:T(8,128)(2,1)}, u32[]{:S(2)}) copy-start(bf16[512,256]{1,0:T(8,128)(2,1)} %constant.27.clone.second_ref) | copy-start | bytes 786436
  27.8 14.3 %copy-start.3 = (bf16[512,256]{1,0:T(8,128)(2,1)S(1)}, bf16[512,256]{1,0:T(8,128)(2,1)}, u32[]{:S(2)}) copy-start(bf16[512,256]{1,0:T(8,128)(2,1)} %constant.32.clone.taps_second_ref) | copy-start | bytes 786436
  27.8 14.3 %copy-start.10 = (bf16[128,144]{1,0:T(8,128)(2,1)S(1)}, bf16[128,144]{1,0:T(8,128)(2,1)}, u32[]{:S(2)}) copy-start(bf16[128,144]{1,0:T(8,128)(2,1)} %constant.28.clone.last_ref) | copy-start | bytes 110596
  28.8 13.3 %copy-start.8 = (bf16[288,64]{1,0:T(8,128)(2,1)S(1)}, bf16[288,64]{1,0:T(8,128)(2,1)}, u32[]{:S(2)}) copy-start(bf16[288,64]{1,0:T(8,128)(2,1)} %constant.25.clone.taps_ref) | copy-start | bytes 110596
